TPU v7x, 512 devices: a whole 4x4x16 slice. The times are simulated.
512 devices in a mesh: row: 16 (over x, y_hi, core), col: 32 (over z, y_lo).
Axes of the slice: x: 4, y: 4 (y_hi: 2, y_lo: 2; y = y_hi * 2 + y_lo), z: 16, core: 2. Of those that a mesh axis runs over, the one named last changes fastest.
Arguments:
- hologram: float32 [2, 512, 32768], P(None, 'row', 'col'), may hold values from -24 to 24
- target: bfloat16 [16, 1024, 4096], P('row', 'col'), may hold values from 0.019897461 to 2
Outputs:
- gradient: float32 [2, 512, 32768], P(None, 'row', 'col')
All inputs are finite; a program needn't handle non-finite values.
Results may differ from a plain program's by a relative error of at most 0.0003.
Values sent between devices are 32-bit elements; how exact they have to be, the bound alone decides.
No kernel may reach another device: no remote copies, remote signals or barrier semaphores. Data moves between devices by JAX's collectives and lax.ppermute only.
A program may use at most 64 MiB of HBM per device.

v0:
```python
import jax
import jax.numpy as jnp
from jax import lax
from jax.sharding import PartitionSpec as P

WIN = 64


def passed_along(block, axis, distance):
    devices = range(lax.axis_size(axis))
    route = [(i - distance, i) for i in devices if i - distance in devices]
    return lax.ppermute(block, axis, route)


def tables():
    indices = jnp.arange(WIN, dtype=jnp.int32)
    phases = (jnp.outer(indices, indices) % WIN).astype(jnp.float32) * (2.0 * jnp.pi / WIN)
    scaling = 1.0 / jnp.sqrt(jnp.float32(WIN))
    cosine = jnp.cos(phases) * scaling
    sines = jnp.sin(phases) * scaling
    ramp = (indices.astype(jnp.float32) + 0.5) * (jnp.pi / WIN)
    profile = jnp.sin(ramp)
    window_taper = profile[:, None] * profile[None, :]
    return (cosine, sines, jnp.concatenate([window_taper, window_taper], axis=1))


def transform(stacked, cosine, sines, sign):
    mixing = jnp.block([[cosine, -sign * sines], [sign * sines, cosine]])
    along_cols = jnp.einsum("wab,bc->wac", stacked, mixing, precision=lax.Precision.HIGHEST)
    cos_part = jnp.einsum("ja,wac->wjc", cosine, along_cols, precision=lax.Precision.HIGHEST)
    sin_part = jnp.einsum("ja,wac->wjc", sines, along_cols, precision=lax.Precision.HIGHEST)
    real_part = cos_part[..., :WIN] + sign * sin_part[..., WIN:]
    imag_part = cos_part[..., WIN:] - sign * sin_part[..., :WIN]
    return jnp.concatenate([real_part, imag_part], axis=-1)


def per_device(hologram, target):
    stride = WIN // 2
    rows_tile = hologram.shape[1]
    cols_tile = hologram.shape[2]
    row_wins = rows_tile // stride
    col_wins = cols_tile // stride
    win_count = row_wins * col_wins
    cell_count = rows_tile * cols_tile * lax.axis_size("row") * lax.axis_size("col")
    cosine, sines, taper_pair = tables()
    energy_local = jnp.sum(hologram * hologram)
    received = passed_along(hologram[:, :, :stride], "col", -1)
    widened = jnp.concatenate([hologram, received], axis=2)
    received_rows = passed_along(widened, "row", -1)
    extended = jnp.concatenate([widened, received_rows], axis=1)
    blocks = extended.reshape(2, row_wins + 1, stride, col_wins + 1, stride)
    upper = jnp.concatenate([blocks[:, :-1, :, :-1], blocks[:, :-1, :, 1:]], axis=4)
    lower = jnp.concatenate([blocks[:, 1:, :, :-1], blocks[:, 1:, :, 1:]], axis=4)
    windows = jnp.concatenate([upper, lower], axis=2)
    windows = windows.transpose(1, 3, 2, 0, 4).reshape(win_count, WIN, 2 * WIN) * taper_pair
    spectrum = transform(windows, cosine, sines, 1.0)
    power = spectrum[..., :WIN] ** 2 + spectrum[..., WIN:] ** 2
    levels = target.reshape(win_count, WIN, WIN).astype(jnp.float32)
    square_local = jnp.sum(power * power)
    cross_local = jnp.sum(levels * power)
    energy_sum, square_sum, cross_sum = lax.psum(
        (energy_local, square_local, cross_local), ("row", "col")
    )
    energy = energy_sum / cell_count + 1e-05
    factor = power / energy - levels
    adjoint = transform(spectrum * jnp.concatenate([factor, factor], axis=-1), cosine, sines, -1.0)
    moment = square_sum / energy - cross_sum
    adjoint = adjoint * taper_pair
    pieces = adjoint.reshape(row_wins, col_wins, WIN, 2, WIN).transpose(3, 0, 2, 1, 4)
    keep_axis = (0, 0)
    grad_grid = jnp.pad(
        pieces[:, :, :stride, :, :stride], (keep_axis, (0, 1), keep_axis, (0, 1), keep_axis)
    )
    grad_grid = grad_grid + jnp.pad(
        pieces[:, :, :stride, :, stride:], (keep_axis, (0, 1), keep_axis, (1, 0), keep_axis)
    )
    grad_grid = grad_grid + jnp.pad(
        pieces[:, :, stride:, :, :stride], (keep_axis, (1, 0), keep_axis, (0, 1), keep_axis)
    )
    grad_grid = grad_grid + jnp.pad(
        pieces[:, :, stride:, :, stride:], (keep_axis, (1, 0), keep_axis, (1, 0), keep_axis)
    )
    grad_grid = grad_grid.reshape(2, rows_tile + stride, cols_tile + stride)
    returned_rows = passed_along(grad_grid[:, rows_tile:, :], "row", 1)
    trimmed = grad_grid[:, :rows_tile, :].at[:, :stride, :].add(returned_rows)
    returned_cols = passed_along(trimmed[:, :, cols_tile:], "col", 1)
    summed_grad = trimmed[:, :, :cols_tile].at[:, :, :stride].add(returned_cols)
    return summed_grad - moment / (energy * energy * cell_count) * hologram


def solution(mesh):
    return jax.shard_map(
        per_device,
        mesh=mesh,
        in_specs=(P(None, "row", "col"), P("row", "col", None)),
        out_specs=P(None, "row", "col"),
        check_vma=False,
    )
```

profile of v0, /device:TPU:1, one launch (start us, length us, event | category | flops | bytes accessed | tf_op | source)
XLA Modules:
  0.0 160.4 jit_solution(14900844122743748685)
XLA Ops:
  0.0 0.8 slice.107
  0.8 1.3 collective-permute-start
  2.0 1.6 %multiply_reduce_fusion.2 = (f32[]{:T(128)}, f32[2,32,1056]{2,1,0:T(8,128)S(1)}) fusion(f32[2,32,1024]{2,1,0:T(8,128)} %param.8), kind=kLoop, calls=%fused_computation.32 | loop fusion | flops 131070 | bytes 524292 | tf_op jit(solution)/shard_map/reduce_sum | solution.py:46
  3.7 0.1 broadcast_multiply_fusion.5
  3.8 0.1 broadcast_multiply_fusion
  3.9 0.1 broadcast_multiply_fusion.2
  4.0 2.1 %collective-permute-done = f32[2,32,32]{2,1,0:T(8,128)S(1)} collective-permute-done((f32[2,32,32]{2,1,0:T(8,128)S(1)}, f32[2,32,32]{2,1,0:T(8,128)S(1)}, u32[]{:S(2)}, u32[]{:S(2)}) %collective-permute-start) | collective-permute-done | bytes 8224 | tf_op jit(solution)/shard_map/ppermute | solution.py:12
  6.1 9.3 %collective-permute-start.1 = (f32[2,32,1056]{2,1,0:T(8,128)S(1)}, f32[2,32,1056]{2,1,0:T(8,128)S(1)}, u32[]{:S(2)}, u32[]{:S(2)}) collective-permute-start(f32[2,32,1056]{2,1,0:T(8,128)S(1)} %constant_dynamic-update-slice_fusion), channel_id=1, source_target_pairs={{32,0},{64,32},{96,64},{128,96},{160,128},{192,160},{224,192},{256... | collective-permute-start | bytes 811016 | tf_op jit(solution)/shard_map/ppermute | solution.py:12
  15.3 0.1 pad_maximum_fusion.9
  15.4 2.3 %reshape.142 = f32[32,64,64]{2,1,0:T(8,128)} reshape(bf16[1,32,4096]{2,1,0:T(8,128)(2,1)} %param.9) | data formatting | bytes 786432 | tf_op jit(solution)/shard_map/convert_element_type | solution.py:58
  17.8 0.2 cosine_multiply_fusion
  17.9 0.0 collective-permute-done.1
  18.0 0.6 reshape.139
  18.6 0.6 fusion.55
  19.3 0.6 maximum_bitcast_fusion
  19.9 1.6 %copy.6 = f32[1,32,64,2,64]{4,3,2,1,0:T(2,128)S(1)} copy(f32[1,32,64,2,64]{4,1,2,0,3:T(8,128)S(1)} %maximum_bitcast_fusion) | data formatting | bytes 2097152 | tf_op jit(solution)/shard_map/transpose | solution.py:55
  21.5 1.1 reshape.140
  22.7 1.0 fusion.9
  23.7 0.0 copy-start
  23.7 1.2 convolution_bitcast_fusion.2
  24.9 1.2 convolution_bitcast_fusion.3
  26.1 0.0 copy-done
  26.1 1.3 multiply_reduce_fusion
  27.4 110.1 %all-reduce.4 = (f32[]{:T(128)}, f32[]{:T(128)}, f32[]{:T(128)}) all-reduce(f32[]{:T(128)} %get-tuple-element.54, f32[]{:T(128)} %get-tuple-element.38, f32[]{:T(128)} %get-tuple-element.37), channel_id=1, replica_groups=mesh['row'=16,'col'=32] {'row','col'}, use_global_device_ids=true, to_apply=%region_1.2 | all-reduce | flops 3 | bytes 24 | tf_op jit(solution)/shard_map/psum | solution.py:61
  138.2 0.3 divide_subtract_fusion
  138.5 1.4 fusion.3
  139.9 1.2 convolution_bitcast_fusion
  141.1 1.2 convolution_bitcast_fusion.1
  142.2 0.6 fusion.2
  142.9 0.3 pad_maximum_fusion
  143.2 1.2 concatenate.72
  144.4 1.2 fusion
  145.6 0.7 fusion.56
  146.4 0.6 pad_add_fusion
  147.0 0.0 copy-start.1
  147.0 0.5 reshape.141
  147.6 3.6 %collective-permute-start.2 = (f32[2,32,1056]{2,1,0:T(8,128)S(1)}, f32[2,32,1056]{2,1,0:T(8,128)S(1)}, u32[]{:S(2)}, u32[]{:S(2)}) collective-permute-start(f32[2,32,1056]{2,1,0:T(8,128)S(1)} %slice.146), channel_id=1, source_target_pairs={{0,32},{32,64},{64,96},{96,128},{128,160},{160,192},{192,224},{224... | collective-permute-start | bytes 811016 | tf_op jit(solution)/shard_map/ppermute | solution.py:12
  151.2 3.6 %collective-permute-done.2 = f32[2,32,1056]{2,1,0:T(8,128)S(1)} collective-permute-done((f32[2,32,1056]{2,1,0:T(8,128)S(1)}, f32[2,32,1056]{2,1,0:T(8,128)S(1)}, u32[]{:S(2)}, u32[]{:S(2)}) %collective-permute-start.2) | collective-permute-done | bytes 270368 | tf_op jit(solution)/shard_map/ppermute | solution.py:12
  154.9 3.1 %collective-permute-start.3 = (f32[2,32,32]{2,1,0:T(8,128)S(1)}, f32[2,32,32]{2,1,0:T(8,128)S(1)}, u32[]{:S(2)}, u32[]{:S(2)}) collective-permute-start(f32[2,32,32]{2,1,0:T(8,128)S(1)} %slice.149), channel_id=1, source_target_pairs={{0,1},{1,2},{2,3},{3,4},{4,5},{5,6},{6,7},{7,8},{8,9},{9,10},{10,1... | collective-permute-start | bytes 24584 | tf_op jit(solution)/shard_map/ppermute | solution.py:12
  159.3 0.0 collective-permute-done.3
  159.3 0.4 scatter-add.4
  159.7 0.0 copy-done.1
  159.7 0.7 multiply_subtract_fusion
  (9 shorter events, 0.2 us)
Async XLA Ops:
  0.8 5.3 %collective-permute-start = (f32[2,32,32]{2,1,0:T(8,128)S(1)}, f32[2,32,32]{2,1,0:T(8,128)S(1)}, u32[]{:S(2)}, u32[]{:S(2)}) collective-permute-start(f32[2,32,32]{2,1,0:T(8,128)S(1)} %slice.107), channel_id=1, source_target_pairs={{1,0},{2,1},{3,2},{4,3},{5,4},{6,5},{7,6},{8,7},{9,8},{10,9},{11,1... | collective-permute-start | bytes 24584 | tf_op jit(solution)/shard_map/ppermute | solution.py:12
  6.1 11.9 %collective-permute-start.1 = (f32[2,32,1056]{2,1,0:T(8,128)S(1)}, f32[2,32,1056]{2,1,0:T(8,128)S(1)}, u32[]{:S(2)}, u32[]{:S(2)}) collective-permute-start(f32[2,32,1056]{2,1,0:T(8,128)S(1)} %constant_dynamic-update-slice_fusion), channel_id=1, source_target_pairs={{32,0},{64,32},{96,64},{128,96},{160,128},{192,160},{224,192},{256... | collective-permute-start | bytes 811016 | tf_op jit(solution)/shard_map/ppermute | solution.py:12
  23.7 2.4 %copy-start = (f32[32,64,64]{2,1,0:T(8,128)S(1)}, f32[32,64,64]{2,1,0:T(8,128)}, u32[]{:S(2)}) copy-start(f32[32,64,64]{2,1,0:T(8,128)} %reshape.142) | copy-start | bytes 1572868
  147.0 12.7 %copy-start.1 = (f32[2,32,1024]{2,1,0:T(8,128)S(1)}, f32[2,32,1024]{2,1,0:T(8,128)}, u32[]{:S(2)}) copy-start(f32[2,32,1024]{2,1,0:T(8,128)} %param.8) | copy-start | bytes 786436
  147.6 7.3 %collective-permute-start.2 = (f32[2,32,1056]{2,1,0:T(8,128)S(1)}, f32[2,32,1056]{2,1,0:T(8,128)S(1)}, u32[]{:S(2)}, u32[]{:S(2)}) collective-permute-start(f32[2,32,1056]{2,1,0:T(8,128)S(1)} %slice.146), channel_id=1, source_target_pairs={{0,32},{32,64},{64,96},{96,128},{128,160},{160,192},{192,224},{224... | collective-permute-start | bytes 811016 | tf_op jit(solution)/shard_map/ppermute | solution.py:12
  154.9 4.4 %collective-permute-start.3 = (f32[2,32,32]{2,1,0:T(8,128)S(1)}, f32[2,32,32]{2,1,0:T(8,128)S(1)}, u32[]{:S(2)}, u32[]{:S(2)}) collective-permute-start(f32[2,32,32]{2,1,0:T(8,128)S(1)} %slice.149), channel_id=1, source_target_pairs={{0,1},{1,2},{2,3},{3,4},{4,5},{5,6},{6,7},{7,8},{8,9},{9,10},{10,1... | collective-permute-start | bytes 24584 | tf_op jit(solution)/shard_map/ppermute | solution.py:12
where the time goes:
time: 163 us; the launch traced here: 160 us
  blocking collectives  110 us (67%)
  starting transfers between devices  17.3 us (11%)
  local copies, waits for them, and re-layouts  9.97 us (6%)
  other arithmetic  8 us (5%)
  matrix products  7.16 us (4%)
  waiting for transfers between devices  5.71 us (4%)
  between operations  2.22 us (1%)
    psum x1, blocking collectives, per_device(): lax.psum((energy_local, square_local, cross_local), ('row', 'col'))  110 us
    ppermute x4, starting transfers between devices, passed_along(): return lax.ppermute(block, axis, route)  17.3 us
    ppermute x4, waiting for transfers between devices, passed_along(): return lax.ppermute(block, axis, route)  5.71 us
  transfers between devices with their start and end apart: 4, of which 2 were waited for; matrix products, arithmetic and copies ran while one was open for 3% of the time, Pallas kernels for 0%

commit v1 on v0

v1 whole, which is shorter than its diff:
```python
import jax
import jax.numpy as jnp
import ml_dtypes
import numpy as np
from jax import lax
from jax.experimental import pallas as pl
from jax.experimental.pallas import tpu as pltpu
from jax.sharding import PartitionSpec as P

WIN = 64
STRIDE = WIN // 2
LANES = 128
AXES = ("row", "col")
DEPTH_BITS = (1, 2, 3, 4)
PLANE_BITS = (0, 5, 6, 7, 8)
LEAD = 11 * 32 + 21
BF16 = jnp.bfloat16
F32 = jnp.float32
CELLS = 512.0 * 32768.0


def split_host(table):
    high = table.astype(np.float32).astype(ml_dtypes.bfloat16)
    low = (table - high.astype(np.float64)).astype(np.float32).astype(ml_dtypes.bfloat16)
    return high, low


def host_tables():
    index = np.arange(WIN)
    phase = (np.outer(index, index) % WIN) * (2.0 * np.pi / WIN)
    taper = np.sin((index + 0.5) * (np.pi / WIN)) / np.sqrt(WIN)
    cosine = np.cos(phase) * taper[None, :]
    sine = np.sin(phase) * taper[None, :]
    upper, lower = slice(0, STRIDE), slice(STRIDE, WIN)
    by_row = np.block(
        [
            [cosine[:, upper], sine[:, upper], cosine[:, lower], sine[:, lower]],
            [-sine[:, upper], cosine[:, upper], -sine[:, lower], cosine[:, lower]],
        ]
    )
    two = np.eye(2)
    by_col = np.block(
        [
            [np.kron(two, cosine.T), np.kron(two, -sine.T)],
            [np.kron(two, sine.T), np.kron(two, cosine.T)],
        ]
    )
    row_high, row_low = split_host(by_row)
    half = 2 * STRIDE
    forward_own = np.concatenate([row_high[:, :half], row_high[:, :half], row_low[:, :half]], axis=1)
    forward_next = np.concatenate([row_high[:, half:], row_high[:, half:], row_low[:, half:]], axis=1)
    adjoint_high, adjoint_low = row_high.T, row_low.T
    backward = np.concatenate([adjoint_high, adjoint_high, adjoint_low], axis=1)
    col_high, col_low = split_host(by_col)
    pick = np.zeros((2, 2, 32, 2, 2, 32, 2, 2, 2), np.float32)
    for j2 in range(2):
        for e in range(2):
            for kk in range(32):
                for kpar in range(2):
                    pick[j2, e, kk, kpar, kpar, kk, j2, :, e] = 1.0
    pick = pick.reshape(256, 512).astype(ml_dtypes.bfloat16)
    wide = np.zeros((128, 64), ml_dtypes.bfloat16)
    return np.concatenate(
        [
            np.concatenate([forward_own, wide], axis=1),
            np.concatenate([forward_next, wide], axis=1),
            backward[:, :256],
            np.concatenate([backward[:, 256:], wide, wide], axis=1),
            col_high, col_low, col_high.T, col_low.T,
            pick[:, :256], pick[:, 256:],
        ],
        axis=0,
    )


TABLE = host_tables()
OWN, NEXT, BACK, BACK_LOW = (slice(k * 128, (k + 1) * 128) for k in range(4))
COL_HIGH, COL_LOW, COL_HIGH_T, COL_LOW_T, PICK_SAME, PICK_OTHER = (slice(512 + k * 256, 768 + k * 256) for k in range(6))


def split(block):
    high = block.astype(BF16)
    return high, (block - high.astype(F32)).astype(BF16)


def mul(left, right):
    return jnp.dot(left, right, preferred_element_type=F32)


def stacked(block):
    high, low = split(block)
    return jnp.concatenate([high, low, high], axis=0)


def local_kernel(holo_ref, target_ref, table_ref, first_ref, levels_ref, partial_ref, energy_ref):
    holo = holo_ref[...]
    first_ref[...] = holo[:, :LANES]
    energy_ref[...] = jnp.sum((holo * holo).reshape(8, 8, 1024), axis=0)
    partial_ref[...] = mul(table_ref[OWN, :192], stacked(holo))
    lane = lax.broadcasted_iota(jnp.int32, (8, LANES), 1)
    row = lax.broadcasted_iota(jnp.int32, (8, LANES), 0)
    side = (row // 2) % 2
    here = (lane // WIN) == side
    same, other = [], []
    for kk in range(32):
        tile = target_ref[:, kk * LANES:(kk + 1) * LANES].astype(F32)
        turned = pltpu.roll(tile, WIN, axis=1)
        parts_same, parts_other = [], []
        for g in range(4):
            plain = tile[8 * g:8 * g + 8]
            moved = turned[8 * g:8 * g + 8]
            parts_same.append(jnp.where(here, jnp.where(side == 0, plain, moved), 0.0))
            parts_other.append(jnp.where(here, jnp.where(side == 0, moved, plain), 0.0))
        same.append(jnp.concatenate(parts_same, axis=1))
        other.append(jnp.concatenate(parts_other, axis=1))
    gathered = jnp.concatenate(same + other, axis=0).astype(BF16)
    placed = mul(table_ref[PICK_SAME, :], gathered[:256]) + mul(table_ref[PICK_OTHER, :], gathered[256:])
    for g in range(4):
        for j2 in range(2):
            for e in range(2):
                start = (e * 8 + 2 * g + j2) * WIN
                source = (j2 * 2 + e) * WIN
                levels_ref[start:start + WIN, :] = placed[source:source + WIN, g * LANES:(g + 1) * LANES]


def window_kernel(
    side_ref, main_ref, levels_ref, energy_ref,
    table_ref,
    own_ref, rows_ref, tail_ref, sums_ref,
    high_ref, low_ref, grid_ref,
):
    main = main_ref[...]
    edge = mul(table_ref[OWN, :192], stacked(side_ref[:WIN])) + mul(
        table_ref[NEXT, :192], stacked(side_ref[WIN:])
    )
    wide = jnp.concatenate([main, edge], axis=1)
    shifted = pltpu.roll(wide, 1152 - STRIDE, axis=1)
    for e, field in enumerate((wide, shifted)):
        high, low = split(field)
        for j in range(8):
            at = slice((e * 8 + j) * WIN, (e * 8 + j + 1) * WIN)
            cols = slice(j * LANES, (j + 1) * LANES)
            for c in range(2):
                to = slice(c * LANES, (c + 1) * LANES)
                high_ref[at, to] = high[c * WIN:(c + 1) * WIN, cols]
                low_ref[at, to] = low[c * WIN:(c + 1) * WIN, cols]
    high, low = high_ref[...], low_ref[...]
    spectrum = mul(high, table_ref[COL_HIGH, :]) + mul(low, table_ref[COL_HIGH, :]) + mul(high, table_ref[COL_LOW, :])
    real, imag = spectrum[:, :LANES], spectrum[:, LANES:]
    power = real * real + imag * imag
    levels = levels_ref[...]
    squares = jnp.sum(power * power)
    crosses = jnp.sum(levels * power)
    energy = jnp.sum(energy_ref[...])
    lane = lax.broadcasted_iota(jnp.int32, (1, LANES), 1)
    sums_ref[...] = jnp.where(lane == 0, energy, jnp.where(lane == 1, squares, crosses))
    for v, factor in enumerate((power, levels)):
        high, low = split(jnp.concatenate([real * factor, imag * factor], axis=1))
        cols = mul(high, table_ref[COL_HIGH_T, :]) + mul(low, table_ref[COL_HIGH_T, :])
        cols = cols + mul(high, table_ref[COL_LOW_T, :])
        for c in range(2):
            at = slice(c * WIN, (c + 1) * WIN)
            lanes = slice(c * LANES, (c + 1) * LANES)
            even = [cols[j * WIN:(j + 1) * WIN, lanes] for j in range(8)]
            odd = [cols[(8 + j) * WIN:(9 + j) * WIN, lanes] for j in range(8)]
            zero = jnp.zeros((WIN, LANES), F32)
            grid_ref[at, :] = jnp.concatenate(even + [zero], axis=1) + pltpu.roll(
                jnp.concatenate(odd + [zero], axis=1), STRIDE, axis=1
            )
        high, low = split(grid_ref[...])
        result = mul(table_ref[BACK, :], jnp.concatenate([high, low], axis=0)) + mul(table_ref[BACK_LOW, :128], high)
        own_ref[v] = result[:WIN, :1024]
        tail_ref[v] = result[:WIN, 1024:]
        rows_ref[v] = result[WIN:, :]


def vmem(count):
    return [pl.BlockSpec(memory_space=pltpu.VMEM)] * count


def local_part(holo, target):
    return pl.pallas_call(
        local_kernel,
        out_shape=(
            jax.ShapeDtypeStruct((WIN, LANES), F32),
            jax.ShapeDtypeStruct((1024, LANES), F32),
            jax.ShapeDtypeStruct((128, 1024), F32),
            jax.ShapeDtypeStruct((8, 1024), F32),
        ),
        in_specs=vmem(3),
        out_specs=tuple(vmem(4)),
        compiler_params=pltpu.CompilerParams(vmem_limit_bytes=24 * 1024 * 1024),
        cost_estimate=pl.CostEstimate(flops=10**8, bytes_accessed=3 * 10**6, transcendentals=0),
        name="local_part",
    )(holo, target, TABLE)


def main_kernel(below_ref, partial_ref, table_ref, main_ref):
    main_ref[...] = partial_ref[...] + mul(table_ref[NEXT, :192], stacked(below_ref[...]))


def main_part(below, partial):
    return pl.pallas_call(
        main_kernel,
        out_shape=jax.ShapeDtypeStruct((128, 1024), F32),
        in_specs=vmem(3),
        out_specs=vmem(1)[0],
        compiler_params=pltpu.CompilerParams(vmem_limit_bytes=16 * 1024 * 1024),
        cost_estimate=pl.CostEstimate(flops=10**8, bytes_accessed=2 * 10**6, transcendentals=0),
        name="main_part",
    )(below, partial, TABLE)


def window_part(*operands):
    return pl.pallas_call(
        window_kernel,
        out_shape=(
            jax.ShapeDtypeStruct((2, WIN, 1024), F32),
            jax.ShapeDtypeStruct((2, WIN, 1152), F32),
            jax.ShapeDtypeStruct((2, WIN, LANES), F32),
            jax.ShapeDtypeStruct((1, LANES), F32),
        ),
        in_specs=vmem(5),
        out_specs=tuple(vmem(4)),
        scratch_shapes=[
            pltpu.VMEM((1024, 256), BF16),
            pltpu.VMEM((1024, 256), BF16),
            pltpu.VMEM((128, 1152), F32),
        ],
        compiler_params=pltpu.CompilerParams(vmem_limit_bytes=32 * 1024 * 1024),
        cost_estimate=pl.CostEstimate(flops=10**9, bytes_accessed=5 * 10**6, transcendentals=0),
        name="window_part",
    )(*operands, TABLE)


def combine_kernel(own_ref, rows_ref, cols_ref, holo_ref, sums_ref, out_ref):
    total = jnp.sum(sums_ref[...], axis=0, keepdims=True)
    energy = total[:, 0:1] / CELLS + 1e-5
    moment = total[:, 1:2] / energy - total[:, 2:3]
    inverse = 1.0 / energy
    slope = moment / (energy * energy * CELLS)
    first = own_ref[0] + rows_ref[0, :, :1024]
    second = own_ref[1] + rows_ref[1, :, :1024]
    out_ref[...] = first * inverse - second - slope * holo_ref[...]
    out_ref[:, :LANES] += cols_ref[0] * inverse - cols_ref[1]


def combine(own, rows, cols, holo, sums):
    return pl.pallas_call(
        combine_kernel,
        out_shape=jax.ShapeDtypeStruct((WIN, 1024), F32),
        in_specs=vmem(5),
        out_specs=vmem(1)[0],
        compiler_params=pltpu.CompilerParams(vmem_limit_bytes=16 * 1024 * 1024),
        cost_estimate=pl.CostEstimate(flops=10**6, bytes_accessed=2 * 10**6, transcendentals=0),
        name="combine",
    )(own, rows, cols, holo, sums)


def moved(block, rows, cols):
    row_size, col_size = lax.axis_size("row"), lax.axis_size("col")
    route = [
        (r * col_size + c, (r + rows) * col_size + c + cols)
        for r in range(row_size)
        for c in range(col_size)
        if 0 <= r + rows < row_size and 0 <= c + cols < col_size
    ]
    return lax.ppermute(block, AXES, route)


def shared(values, bits):
    masks = [0]
    for bit in bits:
        masks = masks + [mask ^ (1 << bit) for mask in masks]
    every = masks[-1]
    order = [mask ^ (LEAD & every) for mask in masks]
    groups = [[base | mask for mask in order] for base in range(512) if base & every == 0]
    copies = jnp.broadcast_to(values[None], (len(masks), 1, LANES))
    return lax.all_to_all(copies, AXES, 0, 0, axis_index_groups=groups, tiled=True)


def per_device(hologram, target):
    holo = hologram.reshape(WIN, 1024)
    below = moved(holo, -1, 0)
    first, levels, partial, energy = local_part(holo, target.reshape(32, 4096))
    side = moved(jnp.concatenate([first, below[:, :LANES]], axis=0), 0, -1)
    main = main_part(below, partial)
    own, rows, tail, sums = window_part(side, main, levels, energy)
    rows = moved(rows, 1, 0)
    sums = jnp.sum(shared(sums, DEPTH_BITS), axis=0)
    rows, sums = lax.optimization_barrier((rows, sums))
    cols = moved(tail + rows[:, :, 1024:], 0, 1)
    sums = shared(sums, PLANE_BITS).reshape(32, LANES)
    return combine(own, rows, cols, holo, sums).reshape(2, STRIDE, 1024)


def solution(mesh):
    return jax.shard_map(
        per_device,
        mesh=mesh,
        in_specs=(P(None, "row", "col"), P("row", "col", None)),
        out_specs=P(None, "row", "col"),
        check_vma=False,
    )
```

time: 163 us -> 57.7 us (0.35); the launches traced: 160 us -> 57.3 us
  blocking collectives: 110 us -> 29.7 us
  other arithmetic: 8 us -> 0.03 us
  matrix products: 7.16 us -> 0 us
  local copies, waits for them, and re-layouts: 9.97 us -> 3.16 us
  Pallas kernels: 0 us -> 4.64 us
  between operations: 2.22 us -> 0.13 us
  starting transfers between devices: 17.3 us -> 15.5 us
    psum x1 -> x0, blocking collectives: 110 us -> none  [per_device(): lax.psum((energy_local, square_local, cross_local), ('row', 'col'))]
    all_to_all x0 -> x2, blocking collectives: none -> 29.7 us  [shared(): lax.all_to_all(copies, AXES, 0, 0, axis_index_groups=groups, tiled=True)]
    dot_general x6 -> x0, matrix products: 7.16 us -> none  [the longest x2 2.44 us: transform(): jnp.einsum('wab,bc->wac', stacked, mixing, precision=lax.Precision.HIGHEST)]
    pallas_call x0 -> x4, Pallas kernels: none -> 4.64 us  [the longest x1 3.04 us: window_part(): pl.pallas_call(window_kernel, out_shape=(jax.ShapeDtypeStruct((2, WIN, 10...]
    unnamed x4 -> x10, local copies, waits for them, and re-layouts: 0.01 us -> 3.13 us
    reduce_sum x2 -> x1, other arithmetic: 2.9 us -> 0.02 us  [per_device(): sums = jnp.sum(shared(sums, DEPTH_BITS), axis=0)]
    convert_element_type x1 -> x0, local copies, waits for them, and re-layouts: 2.35 us -> none  [per_device(): levels = target.reshape(win_count, WIN, WIN).astype(jnp.float32)]
    reshape x3 -> x0, local copies, waits for them, and re-layouts: 2.31 us -> none  [the longest x1 1.13 us: per_device(): windows.transpose(1, 3, 2, 0, 4).reshape(win_count, WIN, 2 * WIN)]
  transfers between devices with their start and end apart: 4 -> 4, of which waited for: 2 -> 1; matrix products, arithmetic and copies ran while one was open for 3% -> 0% of each run, Pallas kernels for 0% -> 1%
where the time goes in v1:
time: 57.7 us; the launch traced here: 57.3 us
  blocking collectives  29.7 us (51%)
  starting transfers between devices  15.5 us (27%)
  Pallas kernels  4.64 us (8%)
  waiting for transfers between devices  4.16 us (7%)
  local copies, waits for them, and re-layouts  3.16 us (5%)
    all_to_all x2, blocking collectives, shared(): lax.all_to_all(copies, AXES, 0, 0, axis_index_groups=groups, tiled=True)  29.7 us
    ppermute x4, starting transfers between devices, moved(): return lax.ppermute(block, AXES, route)  15.5 us
    ppermute x4, waiting for transfers between devices, moved(): return lax.ppermute(block, AXES, route)  4.16 us
    unnamed x10, local copies, waits for them, and re-layouts  3.13 us
    pallas_call x1, Pallas kernels, window_part(): pl.pallas_call(window_kernel, out_shape=(jax.ShapeDtypeStruct((2, WIN, 10...  3.04 us
  transfers between devices with their start and end apart: 4, of which 1 were waited for; matrix products, arithmetic and copies ran while one was open for 0% of the time, Pallas kernels for 1%

profile of v1, /device:TPU:1, one launch (start us, length us, event | category | flops | bytes accessed | tf_op | source)
XLA Modules:
  0.0 57.3 jit_solution(17635903765779158283)
XLA Ops:
  0.0 8.8 %collective-permute-start = (f32[64,1024]{1,0:T(8,128)}, f32[64,1024]{1,0:T(8,128)S(1)}, u32[]{:S(2)}, u32[]{:S(2)}) collective-permute-start(f32[64,1024]{1,0:T(8,128)} %bitcast.8), channel_id=1, source_target_pairs={{32,0},{33,1},{34,2},{35,3},{36,4},{37,5},{38,6},{39,7},{40,8},{41... | collective-permute-start | bytes 786440 | tf_op jit(solution)/shard_map/ppermute | solution.py:268
  8.8 0.0 copy-start
  8.8 1.2 %copy-done = bf16[2048,256]{1,0:T(8,128)(2,1)S(1)} copy-done((bf16[2048,256]{1,0:T(8,128)(2,1)S(1)}, bf16[2048,256]{1,0:T(8,128)(2,1)}, u32[]{:S(2)}) %copy-start) | copy-done | bytes 1048600
  10.0 0.0 copy-start.2
  10.0 0.9 %copy-done.2 = f32[2,32,1024]{2,1,0:T(8,128)S(1)} copy-done((f32[2,32,1024]{2,1,0:T(8,128)S(1)}, f32[2,32,1024]{2,1,0:T(8,128)}, u32[]{:S(2)}) %copy-start.2) | copy-done | bytes 262168
  11.0 0.0 copy-start.4
  11.0 0.9 %copy-done.4 = bf16[1,32,4096]{2,1,0:T(8,128)(2,1)S(1)} copy-done((bf16[1,32,4096]{2,1,0:T(8,128)(2,1)S(1)}, bf16[1,32,4096]{2,1,0:T(8,128)(2,1)}, u32[]{:S(2)}) %copy-start.4) | copy-done | bytes 262168
  11.9 0.4 local_part.1
  12.4 0.0 collective-permute-done.below_ref
  12.4 1.3 %collective-permute-start.1 = (f32[128,128]{1,0:T(8,128)S(1)}, f32[128,128]{1,0:T(8,128)S(1)}, u32[]{:S(2)}, u32[]{:S(2)}) collective-permute-start(f32[128,128]{1,0:T(8,128)S(1)} %pad_maximum_fusion), channel_id=1, source_target_pairs={{1,0},{2,1},{3,2},{4,3},{5,4},{6,5},{7,6},{8,7},{9,8},{10,9},{11,1... | collective-permute-start | bytes 196616 | tf_op jit(solution)/shard_map/ppermute | solution.py:268
  13.7 0.0 copy-start.1
  13.7 0.2 main_part.1.main_ref
  13.9 4.1 %collective-permute-done.1.side_ref = f32[128,128]{1,0:T(8,128)S(1)} collective-permute-done((f32[128,128]{1,0:T(8,128)S(1)}, f32[128,128]{1,0:T(8,128)S(1)}, u32[]{:S(2)}, u32[]{:S(2)}) %collective-permute-start.1) | collective-permute-done | bytes 65568 | tf_op jit(solution)/shard_map/ppermute | solution.py:268
  18.1 0.0 copy-done.1
  18.1 3.0 %window_part.1 = (f32[2,64,1024]{2,1,0:T(8,128)S(1)}, f32[2,64,1152]{2,1,0:T(8,128)S(1)}, f32[2,64,128]{2,1,0:T(8,128)S(1)}, f32[1,128]{1,0:T(1,128)S(1)}) custom-call(f32[128,128]{1,0:T(8,128)S(1)} %collective-permute-done.1.side_ref, f32[128,1024]{1,0:T(8,128)S(1)} %main_part.1.main_ref, f32[1024,128]{1,0:T(8,128)S(1)} %get-tuple-element.17.levels_ref, ...), custom_call_target="tpu_custom_call" | custom-call | flops 1000000000 | bytes 5000000 | tf_op jit(solution)/shard_map/window_part/pallas_call | solution.py:215
  21.1 0.0 copy-start.3
  21.2 2.1 %collective-permute-start.2 = (f32[2,64,1152]{2,1,0:T(8,128)S(1)}, f32[2,64,1152]{2,1,0:T(8,128)S(1)}, u32[]{:S(2)}, u32[]{:S(2)}) collective-permute-start(f32[2,64,1152]{2,1,0:T(8,128)S(1)} %get-tuple-element.20), channel_id=1, source_target_pairs={{0,32},{1,33},{2,34},{3,35},{4,36},{5,37},{6,38},{7,39},{8,40},{9,... | collective-permute-start | bytes 1769480 | tf_op jit(solution)/shard_map/ppermute | solution.py:268
  23.2 18.2 %all_to_all.10 = f32[16,1,128]{2,1,0:T(1,128)S(1)} all-to-all(f32[16,1,128]{2,1,0:T(1,128)S(1)} %broadcast_in_dim.17), channel_id=1, replica_groups={{20,22,16,18,28,30,24,26,4,6,0,2,12,14,8,10},{21,23,17,19,29,31,25,27,5..., dimensions={0} | all-to-all | bytes 16384 | tf_op jit(solution)/shard_map/all_to_all | solution.py:279
  41.4 0.0 collective-permute-done.2.rows_ref
  41.4 3.4 %collective-permute-start.3 = (f32[2,64,128]{2,1,0:T(8,128)S(1)}, f32[2,64,128]{2,1,0:T(8,128)S(1)}, u32[]{:S(2)}, u32[]{:S(2)}) collective-permute-start(f32[2,64,128]{2,1,0:T(8,128)S(1)} %slice_add_fusion), channel_id=1, source_target_pairs={{0,1},{1,2},{2,3},{3,4},{4,5},{5,6},{6,7},{7,8},{8,9},{9,10},{10,1... | collective-permute-start | bytes 196616 | tf_op jit(solution)/shard_map/ppermute | solution.py:268
  44.8 11.6 %all_to_all.11 = f32[32,1,128]{2,1,0:T(1,128)S(1)} all-to-all(f32[32,1,128]{2,1,0:T(1,128)S(1)} %broadcast_in_dim.19), channel_id=1, replica_groups={{353,352,321,320,289,288,257,256,481,480,449,448,417,416,385,384,97,96,..., dimensions={0} | all-to-all | bytes 32768 | tf_op jit(solution)/shard_map/all_to_all | solution.py:279
  56.4 0.0 collective-permute-done.3.cols_ref
  56.4 0.0 copy-done.3
  56.4 0.9 %combine.1 = f32[64,1024]{1,0:T(8,128)} custom-call(f32[2,64,1024]{2,1,0:T(8,128)S(1)} %get-tuple-element.19.own_ref, f32[2,64,1152]{2,1,0:T(8,128)S(1)} %collective-permute-done.2.rows_ref, f32[2,64,128]{2,1,0:T(8,128)S(1)} %collective-permute-done.3.cols_ref, f32[64,1024]{1,0:T(8,128)S(1)} %bitcast.10, f32[32,128]{1,0:T(8,128)S(1)} %bitcast.12), custom_call_target="tpu_custom_call" | custom-call | flops 1000000 | bytes 2000000 | tf_op jit(solution)/shard_map/combine/pallas_call | solution.py:249
  (6 shorter events, 0.1 us)
Async XLA Ops:
  0.0 12.4 %collective-permute-start = (f32[64,1024]{1,0:T(8,128)}, f32[64,1024]{1,0:T(8,128)S(1)}, u32[]{:S(2)}, u32[]{:S(2)}) collective-permute-start(f32[64,1024]{1,0:T(8,128)} %bitcast.8), channel_id=1, source_target_pairs={{32,0},{33,1},{34,2},{35,3},{36,4},{37,5},{38,6},{39,7},{40,8},{41... | collective-permute-start | bytes 786440 | tf_op jit(solution)/shard_map/ppermute | solution.py:268
  8.8 1.2 %copy-start = (bf16[2048,256]{1,0:T(8,128)(2,1)S(1)}, bf16[2048,256]{1,0:T(8,128)(2,1)}, u32[]{:S(2)}) copy-start(bf16[2048,256]{1,0:T(8,128)(2,1)} %constant.4.clone.table_ref) | copy-start | bytes 3145732
  10.0 0.9 %copy-start.2 = (f32[2,32,1024]{2,1,0:T(8,128)S(1)}, f32[2,32,1024]{2,1,0:T(8,128)}, u32[]{:S(2)}) copy-start(f32[2,32,1024]{2,1,0:T(8,128)} %param.3) | copy-start | bytes 786436
  11.0 0.9 %copy-start.4 = (bf16[1,32,4096]{2,1,0:T(8,128)(2,1)S(1)}, bf16[1,32,4096]{2,1,0:T(8,128)(2,1)}, u32[]{:S(2)}) copy-start(bf16[1,32,4096]{2,1,0:T(8,128)(2,1)} %param.4) | copy-start | bytes 786436
  12.4 5.7 %collective-permute-start.1 = (f32[128,128]{1,0:T(8,128)S(1)}, f32[128,128]{1,0:T(8,128)S(1)}, u32[]{:S(2)}, u32[]{:S(2)}) collective-permute-start(f32[128,128]{1,0:T(8,128)S(1)} %pad_maximum_fusion), channel_id=1, source_target_pairs={{1,0},{2,1},{3,2},{4,3},{5,4},{6,5},{7,6},{8,7},{9,8},{10,9},{11,1... | collective-permute-start | bytes 196616 | tf_op jit(solution)/shard_map/ppermute | solution.py:268
  13.7 4.4 %copy-start.1 = (bf16[2048,256]{1,0:T(8,128)(2,1)S(1)}, bf16[2048,256]{1,0:T(8,128)(2,1)}, u32[]{:S(2)}) copy-start(bf16[2048,256]{1,0:T(8,128)(2,1)} %constant.4.clone.table_ref) | copy-start | bytes 3145732
  21.1 35.3 %copy-start.3 = (f32[2,32,1024]{2,1,0:T(8,128)S(1)}, f32[2,32,1024]{2,1,0:T(8,128)}, u32[]{:S(2)}) copy-start(f32[2,32,1024]{2,1,0:T(8,128)} %param.3) | copy-start | bytes 786436
  21.2 20.3 %collective-permute-start.2 = (f32[2,64,1152]{2,1,0:T(8,128)S(1)}, f32[2,64,1152]{2,1,0:T(8,128)S(1)}, u32[]{:S(2)}, u32[]{:S(2)}) collective-permute-start(f32[2,64,1152]{2,1,0:T(8,128)S(1)} %get-tuple-element.20), channel_id=1, source_target_pairs={{0,32},{1,33},{2,34},{3,35},{4,36},{5,37},{6,38},{7,39},{8,40},{9,... | collective-permute-start | bytes 1769480 | tf_op jit(solution)/shard_map/ppermute | solution.py:268
  41.4 15.0 %collective-permute-start.3 = (f32[2,64,128]{2,1,0:T(8,128)S(1)}, f32[2,64,128]{2,1,0:T(8,128)S(1)}, u32[]{:S(2)}, u32[]{:S(2)}) collective-permute-start(f32[2,64,128]{2,1,0:T(8,128)S(1)} %slice_add_fusion), channel_id=1, source_target_pairs={{0,1},{1,2},{2,3},{3,4},{4,5},{5,6},{6,7},{7,8},{8,9},{9,10},{10,1... | collective-permute-start | bytes 196616 | tf_op jit(solution)/shard_map/ppermute | solution.py:268

commit v2 on v1

--- a/solution.py
+++ b/solution.py
@@ -11,12 +11,13 @@
 STRIDE = WIN // 2
 LANES = 128
 AXES = ("row", "col")
-DEPTH_BITS = (1, 2, 3, 4)
-PLANE_BITS = (0, 5, 6, 7, 8)
+DEPTH_BITS = (5, 1, 2, 3, 4)
+PLANE_BITS = (0, 6, 7, 8)
 LEAD = 11 * 32 + 21
 BF16 = jnp.bfloat16
 F32 = jnp.float32
 CELLS = 512.0 * 32768.0
+MERGE_BYTES = 300000
 
 
 def split_host(table):
@@ -92,11 +93,24 @@
     return jnp.concatenate([high, low, high], axis=0)
 
 
-def local_kernel(holo_ref, target_ref, table_ref, first_ref, levels_ref, partial_ref, energy_ref):
+def local_kernel(
+    holo_hbm, target_hbm, table_hbm, holo_ref, table_ref, levels_ref, partial_ref, energy_ref, target_ref, sems
+):
+    copies = [
+        pltpu.make_async_copy(source, place, sems.at[k])
+        for k, (source, place) in enumerate(
+            [(holo_hbm, holo_ref), (table_hbm, table_ref), (target_hbm, target_ref)]
+        )
+    ]
+    for copy in copies:
+        copy.start()
+    copies[0].wait()
     holo = holo_ref[...]
-    first_ref[...] = holo[:, :LANES]
     energy_ref[...] = jnp.sum((holo * holo).reshape(8, 8, 1024), axis=0)
-    partial_ref[...] = mul(table_ref[OWN, :192], stacked(holo))
+    field = stacked(holo)
+    copies[1].wait()
+    partial_ref[...] = mul(table_ref[OWN, :192], field)
+    copies[2].wait()
     lane = lax.broadcasted_iota(jnp.int32, (8, LANES), 1)
     row = lax.broadcasted_iota(jnp.int32, (8, LANES), 0)
     side = (row // 2) % 2
@@ -123,16 +137,18 @@
                 levels_ref[start:start + WIN, :] = placed[source:source + WIN, g * LANES:(g + 1) * LANES]
 
 
+def along_cols(high, low, table_ref, high_at, low_at):
+    table = jnp.concatenate([table_ref[high_at, :], table_ref[high_at, :], table_ref[low_at, :]], axis=0)
+    return mul(jnp.concatenate([high, low, high], axis=1), table)
+
+
 def window_kernel(
-    side_ref, main_ref, levels_ref, energy_ref,
-    table_ref,
-    own_ref, rows_ref, tail_ref, sums_ref,
-    high_ref, low_ref, grid_ref,
+    below_ref, right_ref, corner_ref, table_ref, levels_ref, partial_ref, energy_ref,
+    own_ref, rows_ref, tail_ref, sums_hbm,
+    high_ref, low_ref, grid_ref, copies_ref, sem,
 ):
-    main = main_ref[...]
-    edge = mul(table_ref[OWN, :192], stacked(side_ref[:WIN])) + mul(
-        table_ref[NEXT, :192], stacked(side_ref[WIN:])
-    )
+    main = partial_ref[...] + mul(table_ref[NEXT, :192], stacked(below_ref[...]))
+    edge = mul(table_ref[OWN, :192], stacked(right_ref[...])) + mul(table_ref[NEXT, :192], stacked(corner_ref[...]))
     wide = jnp.concatenate([main, edge], axis=1)
     shifted = pltpu.roll(wide, 1152 - STRIDE, axis=1)
     for e, field in enumerate((wide, shifted)):
@@ -144,8 +160,7 @@
                 to = slice(c * LANES, (c + 1) * LANES)
                 high_ref[at, to] = high[c * WIN:(c + 1) * WIN, cols]
                 low_ref[at, to] = low[c * WIN:(c + 1) * WIN, cols]
-    high, low = high_ref[...], low_ref[...]
-    spectrum = mul(high, table_ref[COL_HIGH, :]) + mul(low, table_ref[COL_HIGH, :]) + mul(high, table_ref[COL_LOW, :])
+    spectrum = along_cols(high_ref[...], low_ref[...], table_ref, COL_HIGH, COL_LOW)
     real, imag = spectrum[:, :LANES], spectrum[:, LANES:]
     power = real * real + imag * imag
     levels = levels_ref[...]
@@ -153,11 +168,12 @@
     crosses = jnp.sum(levels * power)
     energy = jnp.sum(energy_ref[...])
     lane = lax.broadcasted_iota(jnp.int32, (1, LANES), 1)
-    sums_ref[...] = jnp.where(lane == 0, energy, jnp.where(lane == 1, squares, crosses))
+    row = jnp.where(lane == 0, energy, jnp.where(lane == 1, squares, crosses))
+    copies_ref[...] = jnp.broadcast_to(row[None], copies_ref.shape)
+    copy = pltpu.make_async_copy(copies_ref, sums_hbm, sem)
     for v, factor in enumerate((power, levels)):
         high, low = split(jnp.concatenate([real * factor, imag * factor], axis=1))
-        cols = mul(high, table_ref[COL_HIGH_T, :]) + mul(low, table_ref[COL_HIGH_T, :])
-        cols = cols + mul(high, table_ref[COL_LOW_T, :])
+        cols = along_cols(high, low, table_ref, COL_HIGH_T, COL_LOW_T)
         for c in range(2):
             at = slice(c * WIN, (c + 1) * WIN)
             lanes = slice(c * LANES, (c + 1) * LANES)
@@ -167,48 +183,36 @@
             grid_ref[at, :] = jnp.concatenate(even + [zero], axis=1) + pltpu.roll(
                 jnp.concatenate(odd + [zero], axis=1), STRIDE, axis=1
             )
-        high, low = split(grid_ref[...])
-        result = mul(table_ref[BACK, :], jnp.concatenate([high, low], axis=0)) + mul(table_ref[BACK_LOW, :128], high)
+        if v == 1:
+            copy.start()
+        result = mul(jnp.concatenate([table_ref[BACK, :], table_ref[BACK_LOW, :128]], axis=1), stacked(grid_ref[...]))
         own_ref[v] = result[:WIN, :1024]
         tail_ref[v] = result[:WIN, 1024:]
         rows_ref[v] = result[WIN:, :]
+    copy.wait()
 
 
 def vmem(count):
     return [pl.BlockSpec(memory_space=pltpu.VMEM)] * count
 
 
-def local_part(holo, target):
+def local_part(*operands):
     return pl.pallas_call(
         local_kernel,
         out_shape=(
-            jax.ShapeDtypeStruct((WIN, LANES), F32),
-            jax.ShapeDtypeStruct((1024, LANES), F32),
-            jax.ShapeDtypeStruct((128, 1024), F32),
-            jax.ShapeDtypeStruct((8, 1024), F32),
+            pltpu.VMEM((WIN, 1024), F32),
+            pltpu.VMEM(TABLE.shape, BF16),
+            pltpu.VMEM((1024, LANES), F32),
+            pltpu.VMEM((128, 1024), F32),
+            pltpu.VMEM((8, 1024), F32),
         ),
-        in_specs=vmem(3),
-        out_specs=tuple(vmem(4)),
+        in_specs=[pl.BlockSpec(memory_space=pl.ANY)] * 3,
+        out_specs=tuple(vmem(5)),
+        scratch_shapes=[pltpu.VMEM((32, 4096), BF16), pltpu.SemaphoreType.DMA((3,))],
         compiler_params=pltpu.CompilerParams(vmem_limit_bytes=24 * 1024 * 1024),
         cost_estimate=pl.CostEstimate(flops=10**8, bytes_accessed=3 * 10**6, transcendentals=0),
         name="local_part",
-    )(holo, target, TABLE)
-
-
-def main_kernel(below_ref, partial_ref, table_ref, main_ref):
-    main_ref[...] = partial_ref[...] + mul(table_ref[NEXT, :192], stacked(below_ref[...]))
-
-
-def main_part(below, partial):
-    return pl.pallas_call(
-        main_kernel,
-        out_shape=jax.ShapeDtypeStruct((128, 1024), F32),
-        in_specs=vmem(3),
-        out_specs=vmem(1)[0],
-        compiler_params=pltpu.CompilerParams(vmem_limit_bytes=16 * 1024 * 1024),
-        cost_estimate=pl.CostEstimate(flops=10**8, bytes_accessed=2 * 10**6, transcendentals=0),
-        name="main_part",
-    )(below, partial, TABLE)
+    )(*(pltpu.with_memory_space_constraint(operand, pltpu.HBM) for operand in operands))
 
 
 def window_part(*operands):
@@ -218,43 +222,59 @@
             jax.ShapeDtypeStruct((2, WIN, 1024), F32),
             jax.ShapeDtypeStruct((2, WIN, 1152), F32),
             jax.ShapeDtypeStruct((2, WIN, LANES), F32),
-            jax.ShapeDtypeStruct((1, LANES), F32),
+            pltpu.HBM((32, 1, LANES), F32),
         ),
-        in_specs=vmem(5),
-        out_specs=tuple(vmem(4)),
+        in_specs=vmem(7),
+        out_specs=tuple(vmem(3)) + (pl.BlockSpec(memory_space=pl.ANY),),
         scratch_shapes=[
             pltpu.VMEM((1024, 256), BF16),
             pltpu.VMEM((1024, 256), BF16),
             pltpu.VMEM((128, 1152), F32),
+            pltpu.VMEM((32, 1, LANES), F32),
+            pltpu.SemaphoreType.DMA,
         ],
         compiler_params=pltpu.CompilerParams(vmem_limit_bytes=32 * 1024 * 1024),
         cost_estimate=pl.CostEstimate(flops=10**9, bytes_accessed=5 * 10**6, transcendentals=0),
         name="window_part",
-    )(*operands, TABLE)
-
-
-def combine_kernel(own_ref, rows_ref, cols_ref, holo_ref, sums_ref, out_ref):
+    )(*operands)
+
+
+def merge_kernel(own_ref, rows_ref, both_ref):
+    both_ref[...] = own_ref[...] + rows_ref[:, :, :1024]
+
+
+def merge_part(own, rows):
+    return pl.pallas_call(
+        merge_kernel,
+        out_shape=pltpu.VMEM((2, WIN, 1024), F32),
+        in_specs=vmem(2),
+        out_specs=vmem(1)[0],
+        compiler_params=pltpu.CompilerParams(vmem_limit_bytes=16 * 1024 * 1024),
+        cost_estimate=pl.CostEstimate(flops=10**6, bytes_accessed=MERGE_BYTES, transcendentals=0),
+        name="merge_part",
+    )(own, rows)
+
+
+def combine_kernel(both_ref, edge_ref, holo_ref, sums_ref, out_ref):
     total = jnp.sum(sums_ref[...], axis=0, keepdims=True)
     energy = total[:, 0:1] / CELLS + 1e-5
     moment = total[:, 1:2] / energy - total[:, 2:3]
     inverse = 1.0 / energy
     slope = moment / (energy * energy * CELLS)
-    first = own_ref[0] + rows_ref[0, :, :1024]
-    second = own_ref[1] + rows_ref[1, :, :1024]
-    out_ref[...] = first * inverse - second - slope * holo_ref[...]
-    out_ref[:, :LANES] += cols_ref[0] * inverse - cols_ref[1]
-
-
-def combine(own, rows, cols, holo, sums):
+    out_ref[...] = both_ref[0] * inverse - both_ref[1] - slope * holo_ref[...]
+    out_ref[:, :LANES] += edge_ref[0] * inverse - edge_ref[1]
+
+
+def combine(*operands):
     return pl.pallas_call(
         combine_kernel,
         out_shape=jax.ShapeDtypeStruct((WIN, 1024), F32),
-        in_specs=vmem(5),
+        in_specs=vmem(4),
         out_specs=vmem(1)[0],
         compiler_params=pltpu.CompilerParams(vmem_limit_bytes=16 * 1024 * 1024),
         cost_estimate=pl.CostEstimate(flops=10**6, bytes_accessed=2 * 10**6, transcendentals=0),
         name="combine",
-    )(own, rows, cols, holo, sums)
+    )(*operands)
 
 
 def moved(block, rows, cols):
@@ -275,23 +295,27 @@
     every = masks[-1]
     order = [mask ^ (LEAD & every) for mask in masks]
     groups = [[base | mask for mask in order] for base in range(512) if base & every == 0]
-    copies = jnp.broadcast_to(values[None], (len(masks), 1, LANES))
+    copies = values
+    if copies.ndim == 2:
+        copies = jnp.broadcast_to(values[None], (len(masks), 1, LANES))
     return lax.all_to_all(copies, AXES, 0, 0, axis_index_groups=groups, tiled=True)
 
 
 def per_device(hologram, target):
     holo = hologram.reshape(WIN, 1024)
     below = moved(holo, -1, 0)
-    first, levels, partial, energy = local_part(holo, target.reshape(32, 4096))
-    side = moved(jnp.concatenate([first, below[:, :LANES]], axis=0), 0, -1)
-    main = main_part(below, partial)
-    own, rows, tail, sums = window_part(side, main, levels, energy)
+    first = holo[:, :LANES]
+    corner = moved(first, -1, -1)
+    right = moved(first, 0, -1)
+    holo, *local = local_part(holo, target.reshape(32, 4096), TABLE)
+    own, rows, tail, sums = window_part(below, right, corner, *local)
     rows = moved(rows, 1, 0)
+    edge = moved(tail + rows[:, :, 1024:], 0, 1)
     sums = jnp.sum(shared(sums, DEPTH_BITS), axis=0)
-    rows, sums = lax.optimization_barrier((rows, sums))
-    cols = moved(tail + rows[:, :, 1024:], 0, 1)
-    sums = shared(sums, PLANE_BITS).reshape(32, LANES)
-    return combine(own, rows, cols, holo, sums).reshape(2, STRIDE, 1024)
+    both = merge_part(own, rows)
+    both, sums = lax.optimization_barrier((both, sums))
+    sums = shared(sums, PLANE_BITS).reshape(-1, LANES)
+    return combine(both, edge, holo, sums).reshape(2, STRIDE, 1024)
 
 
 def solution(mesh):

time: 57.7 us -> 53.5 us (0.927)
  blocking collectives: 29.7 us -> 10.1 us
  starting transfers between devices: 15.5 us -> 32.1 us
  local copies, waits for them, and re-layouts: 3.16 us -> 0.77 us
  Pallas kernels: 4.64 us -> 6.38 us
  waiting for transfers between devices: 4.16 us -> 3.3 us
    all_to_all x2 -> x1, blocking collectives: 29.7 us -> 10.1 us  [shared(): lax.all_to_all(copies, AXES, 0, 0, axis_index_groups=groups, tiled=True)]
    all_to_all x0 -> x1, starting transfers between devices: none -> 12.7 us  [shared(): lax.all_to_all(copies, AXES, 0, 0, axis_index_groups=groups, tiled=True)]
    ppermute x4 -> x5, starting transfers between devices: 15.5 us -> 19.4 us  [moved(): return lax.ppermute(block, AXES, route)]
    unnamed x10 -> x0, local copies, waits for them, and re-layouts: 3.13 us -> none
    ppermute x4 -> x5, waiting for transfers between devices: 4.16 us -> 1.88 us  [moved(): return lax.ppermute(block, AXES, route)]
    all_to_all x0 -> x1, waiting for transfers between devices: none -> 1.42 us  [shared(): lax.all_to_all(copies, AXES, 0, 0, axis_index_groups=groups, tiled=True)]
    pallas_call x2, Pallas kernels: 0.66 us -> 2.02 us  [the longest x1 1.97 us: local_part(): pl.pallas_call(local_kernel, out_shape=(pltpu.VMEM((WIN, 1024), F32), plt...]
    slice x1, local copies, waits for them, and re-layouts: 0.01 us -> 0.76 us  [per_device(): first = holo[:, :LANES]]
  transfers between devices with their start and end apart: 4 -> 6, of which waited for: 1 -> 2; matrix products, arithmetic and copies ran while one was open for 0% -> 2% of each run, Pallas kernels for 1% -> 4%
where the time goes in v2:
time: 53.5 us; the launch traced here: 52.9 us
  starting transfers between devices  32.1 us (60%)
  blocking collectives  10.1 us (19%)
  Pallas kernels  6.38 us (12%)
  waiting for transfers between devices  3.3 us (6%)
  local copies, waits for them, and re-layouts  0.77 us (1%)
    ppermute x5, starting transfers between devices, moved(): return lax.ppermute(block, AXES, route)  19.4 us
    all_to_all x1, starting transfers between devices, shared(): lax.all_to_all(copies, AXES, 0, 0, axis_index_groups=groups, tiled=True)  12.7 us
    all_to_all x1, blocking collectives, shared(): lax.all_to_all(copies, AXES, 0, 0, axis_index_groups=groups, tiled=True)  10.1 us
    pallas_call x1, Pallas kernels, window_part(): pl.pallas_call(window_kernel, out_shape=(jax.ShapeDtypeStruct((2, WIN, 10...  3.42 us
    pallas_call x1, Pallas kernels, local_part(): pl.pallas_call(local_kernel, out_shape=(pltpu.VMEM((WIN, 1024), F32), plt...  1.97 us
    ppermute x5, waiting for transfers between devices, moved(): return lax.ppermute(block, AXES, route)  1.88 us
    all_to_all x1, waiting for transfers between devices, shared(): lax.all_to_all(copies, AXES, 0, 0, axis_index_groups=groups, tiled=True)  1.42 us
  transfers between devices with their start and end apart: 6, of which 2 were waited for; matrix products, arithmetic and copies ran while one was open for 2% of the time, Pallas kernels for 4%

profile of v2, /device:TPU:1, one launch (start us, length us, event | category | flops | bytes accessed | tf_op | source)
XLA Modules:
  0.0 52.9 jit_solution(8083339015320863000)
XLA Ops:
  0.0 8.8 %collective-permute-start = (f32[64,1024]{1,0:T(8,128)}, f32[64,1024]{1,0:T(8,128)S(1)}, u32[]{:S(2)}, u32[]{:S(2)}) collective-permute-start(f32[64,1024]{1,0:T(8,128)} %bitcast.7), channel_id=1, source_target_pairs={{32,0},{33,1},{34,2},{35,3},{36,4},{37,5},{38,6},{39,7},{40,8},{41... | collective-permute-start | bytes 786440 | tf_op jit(solution)/shard_map/ppermute | solution.py:288
  8.8 0.8 %slice.8 = f32[64,128]{1,0:T(8,128)S(1)} slice(f32[64,1024]{1,0:T(8,128)} %bitcast.8), slice={[0:64], [0:128]} | slice | bytes 65536 | tf_op jit(solution)/shard_map/slice | solution.py:307
  9.5 1.3 %collective-permute-start.2 = (f32[64,128]{1,0:T(8,128)S(1)}, f32[64,128]{1,0:T(8,128)S(1)}, u32[]{:S(2)}, u32[]{:S(2)}) collective-permute-start(f32[64,128]{1,0:T(8,128)S(1)} %slice.8), channel_id=1, source_target_pairs={{33,0},{34,1},{35,2},{36,3},{37,4},{38,5},{39,6},{40,7},{41,8},{42... | collective-permute-start | bytes 98312 | tf_op jit(solution)/shard_map/ppermute | solution.py:288
  10.8 1.3 %collective-permute-start.1 = (f32[64,128]{1,0:T(8,128)S(1)}, f32[64,128]{1,0:T(8,128)S(1)}, u32[]{:S(2)}, u32[]{:S(2)}) collective-permute-start(f32[64,128]{1,0:T(8,128)S(1)} %slice.8), channel_id=1, source_target_pairs={{1,0},{2,1},{3,2},{4,3},{5,4},{6,5},{7,6},{8,7},{9,8},{10,9},{11,1... | collective-permute-start | bytes 98312 | tf_op jit(solution)/shard_map/ppermute | solution.py:288
  12.1 2.0 %local_part.1 = (f32[64,1024]{1,0:T(8,128)S(1)}, bf16[2048,256]{1,0:T(8,128)(2,1)S(1)}, f32[1024,128]{1,0:T(8,128)S(1)}, f32[128,1024]{1,0:T(8,128)S(1)}, f32[8,1024]{1,0:T(8,128)S(1)}) custom-call(f32[64,1024]{1,0:T(8,128)} %bitcast.9, bf16[32,4096]{1,0:T(8,128)(2,1)} %bitcast.10, bf16[2048,256]{1,0:T(8,128)(2,1)} %constant.4.clone.table_hbm), custom_call_target="tpu_custom_call" | custom-call | flops 100000000 | bytes 3000000 | tf_op jit(solution)/shard_map/local_part/pallas_call | solution.py:200
  14.1 1.9 %collective-permute-done.2.corner_ref = f32[64,128]{1,0:T(8,128)S(1)} collective-permute-done((f32[64,128]{1,0:T(8,128)S(1)}, f32[64,128]{1,0:T(8,128)S(1)}, u32[]{:S(2)}, u32[]{:S(2)}) %collective-permute-start.2) | collective-permute-done | bytes 32800 | tf_op jit(solution)/shard_map/ppermute | solution.py:288
  16.0 0.0 collective-permute-done.1.right_ref
  16.0 0.0 collective-permute-done.below_ref
  16.0 3.4 %window_part.1 = (f32[2,64,1024]{2,1,0:T(8,128)S(1)}, f32[2,64,1152]{2,1,0:T(8,128)S(1)}, f32[2,64,128]{2,1,0:T(8,128)S(1)}, f32[32,1,128]{2,1,0:T(1,128)}) custom-call(f32[64,1024]{1,0:T(8,128)S(1)} %collective-permute-done.below_ref, f32[64,128]{1,0:T(8,128)S(1)} %collective-permute-done.1.right_ref, f32[64,128]{1,0:T(8,128)S(1)} %collective-permute-done.2.corner_ref, ...), custom_call_target="tpu_custom_call" | custom-call | flops 1000000000 | bytes 5000000 | tf_op jit(solution)/shard_map/window_part/pallas_call | solution.py:219
  19.4 5.6 %collective-permute-start.3 = (f32[2,64,1152]{2,1,0:T(8,128)S(1)}, f32[2,64,1152]{2,1,0:T(8,128)S(1)}, u32[]{:S(2)}, u32[]{:S(2)}) collective-permute-start(f32[2,64,1152]{2,1,0:T(8,128)S(1)} %get-tuple-element.21), channel_id=1, source_target_pairs={{0,32},{1,33},{2,34},{3,35},{4,36},{5,37},{6,38},{7,39},{8,40},{9,... | collective-permute-start | bytes 1769480 | tf_op jit(solution)/shard_map/ppermute | solution.py:288
  25.0 12.7 %all-to-all-start = ((f32[32,1,128]{2,1,0:T(1,128)}), f32[32,1,128]{2,1,0:T(1,128)S(1)}, u32[]{:S(2)}, u32[]{:S(2)}) async-start(f32[32,1,128]{2,1,0:T(1,128)} %get-tuple-element.22), calls=%async_computation | async-start | bytes 32768 | tf_op jit(solution)/shard_map/all_to_all | solution.py:301
  37.7 0.0 collective-permute-done.3.rows_ref
  37.7 2.5 %collective-permute-start.4 = (f32[2,64,128]{2,1,0:T(8,128)S(1)}, f32[2,64,128]{2,1,0:T(8,128)S(1)}, u32[]{:S(2)}, u32[]{:S(2)}) collective-permute-start(f32[2,64,128]{2,1,0:T(8,128)S(1)} %slice_add_fusion), channel_id=1, source_target_pairs={{0,1},{1,2},{2,3},{3,4},{4,5},{5,6},{6,7},{7,8},{8,9},{9,10},{10,1... | collective-permute-start | bytes 196616 | tf_op jit(solution)/shard_map/ppermute | solution.py:288
  40.2 1.4 %all-to-all-done = f32[32,1,128]{2,1,0:T(1,128)S(1)} async-done(((f32[32,1,128]{2,1,0:T(1,128)}), f32[32,1,128]{2,1,0:T(1,128)S(1)}, u32[]{:S(2)}, u32[]{:S(2)}) %all-to-all-start) | async-done | bytes 16416 | tf_op jit(solution)/shard_map/all_to_all | solution.py:301
  41.7 0.1 reduce_sum.11
  41.7 0.1 merge_part.1.both_ref
  41.8 10.1 %all_to_all.10 = f32[16,1,128]{2,1,0:T(1,128)S(1)} all-to-all(f32[16,1,128]{2,1,0:T(1,128)S(1)} %broadcast_in_dim.9), channel_id=1, replica_groups={{321,320,257,256,449,448,385,384,65,64,1,0,193,192,129,128},{323,322,25..., dimensions={0} | all-to-all | bytes 16384 | tf_op jit(solution)/shard_map/all_to_all | solution.py:301
  51.9 0.0 collective-permute-done.4.edge_ref
  51.9 0.9 %combine.1 = f32[64,1024]{1,0:T(8,128)} custom-call(f32[2,64,1024]{2,1,0:T(8,128)S(1)} %merge_part.1.both_ref, f32[2,64,128]{2,1,0:T(8,128)S(1)} %collective-permute-done.4.edge_ref, f32[64,1024]{1,0:T(8,128)S(1)} %get-tuple-element.25.holo_ref, f32[16,128]{1,0:T(8,128)S(1)} %bitcast.6), custom_call_target="tpu_custom_call" | custom-call | flops 1000000 | bytes 2000000 | tf_op jit(solution)/shard_map/combine/pallas_call | solution.py:269
  (2 shorter events, 0.0 us)
Async XLA Ops:
  0.0 16.0 %collective-permute-start = (f32[64,1024]{1,0:T(8,128)}, f32[64,1024]{1,0:T(8,128)S(1)}, u32[]{:S(2)}, u32[]{:S(2)}) collective-permute-start(f32[64,1024]{1,0:T(8,128)} %bitcast.7), channel_id=1, source_target_pairs={{32,0},{33,1},{34,2},{35,3},{36,4},{37,5},{38,6},{39,7},{40,8},{41... | collective-permute-start | bytes 786440 | tf_op jit(solution)/shard_map/ppermute | solution.py:288
  9.5 6.4 %collective-permute-start.2 = (f32[64,128]{1,0:T(8,128)S(1)}, f32[64,128]{1,0:T(8,128)S(1)}, u32[]{:S(2)}, u32[]{:S(2)}) collective-permute-start(f32[64,128]{1,0:T(8,128)S(1)} %slice.8), channel_id=1, source_target_pairs={{33,0},{34,1},{35,2},{36,3},{37,4},{38,5},{39,6},{40,7},{41,8},{42... | collective-permute-start | bytes 98312 | tf_op jit(solution)/shard_map/ppermute | solution.py:288
  10.8 5.1 %collective-permute-start.1 = (f32[64,128]{1,0:T(8,128)S(1)}, f32[64,128]{1,0:T(8,128)S(1)}, u32[]{:S(2)}, u32[]{:S(2)}) collective-permute-start(f32[64,128]{1,0:T(8,128)S(1)} %slice.8), channel_id=1, source_target_pairs={{1,0},{2,1},{3,2},{4,3},{5,4},{6,5},{7,6},{8,7},{9,8},{10,9},{11,1... | collective-permute-start | bytes 98312 | tf_op jit(solution)/shard_map/ppermute | solution.py:288
  19.4 18.3 %collective-permute-start.3 = (f32[2,64,1152]{2,1,0:T(8,128)S(1)}, f32[2,64,1152]{2,1,0:T(8,128)S(1)}, u32[]{:S(2)}, u32[]{:S(2)}) collective-permute-start(f32[2,64,1152]{2,1,0:T(8,128)S(1)} %get-tuple-element.21), channel_id=1, source_target_pairs={{0,32},{1,33},{2,34},{3,35},{4,36},{5,37},{6,38},{7,39},{8,40},{9,... | collective-permute-start | bytes 1769480 | tf_op jit(solution)/shard_map/ppermute | solution.py:288
  25.0 16.7 %all-to-all-start = ((f32[32,1,128]{2,1,0:T(1,128)}), f32[32,1,128]{2,1,0:T(1,128)S(1)}, u32[]{:S(2)}, u32[]{:S(2)}) async-start(f32[32,1,128]{2,1,0:T(1,128)} %get-tuple-element.22), calls=%async_computation | async-start | bytes 32768 | tf_op jit(solution)/shard_map/all_to_all | solution.py:301
  37.7 14.2 %collective-permute-start.4 = (f32[2,64,128]{2,1,0:T(8,128)S(1)}, f32[2,64,128]{2,1,0:T(8,128)S(1)}, u32[]{:S(2)}, u32[]{:S(2)}) collective-permute-start(f32[2,64,128]{2,1,0:T(8,128)S(1)} %slice_add_fusion), channel_id=1, source_target_pairs={{0,1},{1,2},{2,3},{3,4},{4,5},{5,6},{6,7},{7,8},{8,9},{9,10},{10,1... | collective-permute-start | bytes 196616 | tf_op jit(solution)/shard_map/ppermute | solution.py:288

commit v3 on v2

v3 whole, which is shorter than its diff:
```python
import jax
import jax.numpy as jnp
import ml_dtypes
import numpy as np
from jax import lax
from jax.experimental import pallas as pl
from jax.experimental.pallas import tpu as pltpu
from jax.sharding import PartitionSpec as P

WIN = 64
STRIDE = WIN // 2
LANES = 128
AXES = ("row", "col")
DEPTH_BITS = (5, 1, 2, 3, 4)
PLANE_BITS = (0, 6, 7, 8)
LEAD = 11 * 32 + 21
BF16 = jnp.bfloat16
F32 = jnp.float32
CELLS = 512.0 * 32768.0
INNER = 15 * WIN
MERGE_BYTES = 300000
ZERO_FLOPS = 10**10


def split_host(table):
    high = table.astype(np.float32).astype(ml_dtypes.bfloat16)
    low = (table - high.astype(np.float64)).astype(np.float32).astype(ml_dtypes.bfloat16)
    return high, low


def host_tables():
    index = np.arange(WIN)
    phase = (np.outer(index, index) % WIN) * (2.0 * np.pi / WIN)
    taper = np.sin((index + 0.5) * (np.pi / WIN)) / np.sqrt(WIN)
    cosine = np.cos(phase) * taper[None, :]
    sine = np.sin(phase) * taper[None, :]
    upper, lower = slice(0, STRIDE), slice(STRIDE, WIN)
    by_row = np.block(
        [
            [cosine[:, upper], sine[:, upper], cosine[:, lower], sine[:, lower]],
            [-sine[:, upper], cosine[:, upper], -sine[:, lower], cosine[:, lower]],
        ]
    )
    two = np.eye(2)
    by_col = np.block(
        [
            [np.kron(two, cosine.T), np.kron(two, -sine.T)],
            [np.kron(two, sine.T), np.kron(two, cosine.T)],
        ]
    )
    row_high, row_low = split_host(by_row)
    half = 2 * STRIDE
    col_high, col_low = split_host(by_col)
    return np.concatenate(
        [
            two_level(row_high[:, :half], row_low[:, :half], 256),
            two_level(row_high[:, half:], row_low[:, half:], 256),
            two_level(row_high, row_low, 256),
            two_level(row_high.T, row_low.T, 256),
            col_high, col_low,
        ],
        axis=0,
    )


def two_level(high, low, width):
    pad = np.zeros((high.shape[0], width - 2 * high.shape[1]), high.dtype)
    upper = np.concatenate([high, high, pad], axis=1)
    lower = np.concatenate([low, np.zeros_like(low), pad], axis=1)
    return np.concatenate([upper, lower], axis=0)


TABLE = host_tables()
OWN, NEXT, BOTH, BACK, COL_HIGH, COL_LOW = (slice(k * 256, (k + 1) * 256) for k in range(6))


def split(block):
    high = block.astype(BF16)
    return high, (block - high.astype(F32)).astype(BF16)


def mul(left, right):
    return jnp.dot(left, right, preferred_element_type=F32)


def by_rows(table, block):
    high, low = split(block)
    both = mul(table, jnp.concatenate([high, low], axis=0))
    return both[:128] + both[128:]


def turned(tiles):
    lane = lax.broadcasted_iota(jnp.int32, tiles[0].shape, 1)
    moved_tiles = [pltpu.roll(tile, STRIDE, axis=1) for tile in tiles]
    zero = jnp.zeros_like(tiles[0])
    return [
        jnp.where(lane < STRIDE, before, after)
        for before, after in zip([zero] + moved_tiles, moved_tiles + [zero])
    ]


def zero_kernel(out_ref):
    out_ref[...] = jnp.zeros_like(out_ref)


def zero_part():
    return pl.pallas_call(
        zero_kernel,
        out_shape=pltpu.VMEM((8, LANES), F32),
        out_specs=vmem(1)[0],
        compiler_params=pltpu.CompilerParams(vmem_limit_bytes=16 * 1024 * 1024),
        cost_estimate=pl.CostEstimate(flops=ZERO_FLOPS, bytes_accessed=4096, transcendentals=0),
        name="zero_part",
    )()


def first_kernel(holo_ref, zero_ref, out_ref):
    out_ref[...] = holo_ref[:, :LANES]


def first_part(holo, zero):
    return pl.pallas_call(
        first_kernel,
        out_shape=pltpu.VMEM((WIN, LANES), F32),
        in_specs=vmem(2),
        out_specs=vmem(1)[0],
        compiler_params=pltpu.CompilerParams(vmem_limit_bytes=16 * 1024 * 1024),
        cost_estimate=pl.CostEstimate(flops=0, bytes_accessed=4 * 10**5, transcendentals=0),
        name="first_part",
    )(holo, zero)


def local_kernel(holo_ref, target_ref, table_ref, levels_ref, partial_ref, energy_ref):
    pick = jnp.concatenate(picks(), axis=1)
    holo = holo_ref[...]
    energy = jnp.sum((holo * holo).reshape(8, 8, 1024), axis=0)
    energy_ref[...] = sum(energy[:, k * LANES:(k + 1) * LANES] for k in range(8))
    partial_ref[...] = by_rows(table_ref[OWN, :128], holo)
    lane = lax.broadcasted_iota(jnp.int32, (8, LANES), 1)
    row = lax.broadcasted_iota(jnp.int32, (8, LANES), 0)
    side = (row // 2) % 2
    here = (lane // WIN) == side
    same, other = [], []
    for kk in range(32):
        tile = target_ref[:, kk * LANES:(kk + 1) * LANES].astype(F32)
        turned = pltpu.roll(tile, WIN, axis=1)
        parts_same, parts_other = [], []
        for g in range(4):
            plain = tile[8 * g:8 * g + 8]
            moved = turned[8 * g:8 * g + 8]
            parts_same.append(jnp.where(here, jnp.where(side == 0, plain, moved), 0.0))
            parts_other.append(jnp.where(here, jnp.where(side == 0, moved, plain), 0.0))
        same.append(jnp.concatenate(parts_same, axis=1))
        other.append(jnp.concatenate(parts_other, axis=1))
    gathered = jnp.concatenate(same + other, axis=0).astype(BF16)
    placed = mul(pick, gathered)
    for g in range(4):
        for j2 in range(2):
            for e in range(2):
                start = (e * 8 + 2 * g + j2) * WIN
                source = (j2 * 2 + e) * WIN
                levels_ref[start:start + WIN, :] = placed[source:source + WIN, g * LANES:(g + 1) * LANES]


def along_cols(high, low, table_ref):
    table = jnp.concatenate([table_ref[COL_HIGH, :], table_ref[COL_HIGH, :], table_ref[COL_LOW, :]], axis=0)
    return mul(jnp.concatenate([high, low, high], axis=1), table)


def back_cols(high, low, table_ref):
    table = jnp.concatenate([table_ref[COL_HIGH, :], table_ref[COL_HIGH, :], table_ref[COL_LOW, :]], axis=1)
    fields = jnp.concatenate([high, low, high], axis=1)
    return lax.dot_general(fields, table, (((1,), (1,)), ((), ())), preferred_element_type=F32)


def picks():
    row = lax.broadcasted_iota(jnp.int32, (256, 256), 0)
    col = lax.broadcasted_iota(jnp.int32, (256, 256), 1)
    match = ((row >> 1) & 31) == (col >> 3)
    match = match & ((row >> 7) == ((col >> 2) & 1)) & (((row >> 6) & 1) == (col & 1))
    even = (row & 1) == 0
    return [jnp.where(match & side, 1.0, 0.0).astype(BF16) for side in (even, jnp.logical_not(even))]


def packed(*terms):
    sublane = lax.broadcasted_iota(jnp.int32, (8, LANES), 0)
    lane = lax.broadcasted_iota(jnp.int32, (8, LANES), 1)
    stack = jnp.zeros((8, LANES), F32)
    for k, term in enumerate(terms):
        stack = jnp.where(sublane == k, jnp.sum(term, axis=0, keepdims=True), stack)
    totals = jnp.sum(stack, axis=1, keepdims=True)
    return jnp.sum(jnp.where(lane == sublane, totals, 0.0), axis=0, keepdims=True)


def spread(fields, high_ref, low_ref, first):
    for j, field in enumerate(fields):
        at = slice((first + j) * WIN, (first + j + 1) * WIN)
        high, low = split(field)
        for c in range(2):
            to = slice(c * LANES, (c + 1) * LANES)
            high_ref[at, to] = high[c * WIN:(c + 1) * WIN]
            low_ref[at, to] = low[c * WIN:(c + 1) * WIN]


def back_by_stride(tiles):
    lane = lax.broadcasted_iota(jnp.int32, tiles[0].shape, 1)
    ahead = [pltpu.roll(tile, LANES - STRIDE, axis=1) for tile in tiles]
    return [jnp.where(lane < LANES - STRIDE, here, after) for here, after in zip(ahead[:-1], ahead[1:])]


def spectra(high_ref, low_ref, levels, table_ref):
    spectrum = along_cols(high_ref[...], low_ref[...], table_ref)
    real, imag = spectrum[:, :LANES], spectrum[:, LANES:]
    power = real * real + imag * imag
    return real, imag, power, packed(power * power, levels * power)


def adjoint_cols(real, imag, factor, table_ref):
    high, low = split(jnp.concatenate([real * factor, imag * factor], axis=1))
    return back_cols(high, low, table_ref)


def place(grid_ref, c, tile, at):
    high, low = split(tile)
    grid_ref[c * WIN:(c + 1) * WIN, at:at + LANES] = high
    grid_ref[128 + c * WIN:128 + (c + 1) * WIN, at:at + LANES] = low


def along_rows(grid_ref, table_ref):
    result = mul(table_ref[BACK, :], grid_ref[...])
    return result[:128] + result[128:]


def inner_kernel(
    below_ref, table_ref, levels_ref, partial_ref,
    own_ref, rows_ref, last_ref, sums_ref,
    high_ref, low_ref, grid_ref,
):
    main = partial_ref[...] + by_rows(table_ref[NEXT, :128], below_ref[...])
    tiles = [main[:, j * LANES:(j + 1) * LANES] for j in range(8)]
    last_ref[...] = tiles[7]
    spread(tiles, high_ref, low_ref, 0)
    spread(back_by_stride(tiles), high_ref, low_ref, 8)
    levels = levels_ref[:INNER, :]
    real, imag, power, sums_ref[...] = spectra(high_ref, low_ref, levels, table_ref)
    for v, factor in enumerate((power, levels)):
        cols = adjoint_cols(real, imag, factor, table_ref)
        for c in range(2):
            lanes = slice(c * LANES, (c + 1) * LANES)
            odd = turned([cols[(8 + j) * WIN:(9 + j) * WIN, lanes] for j in range(7)])
            for j in range(8):
                place(grid_ref, c, odd[j] + cols[j * WIN:(j + 1) * WIN, lanes], (v * 8 + j) * LANES)
    result = along_rows(grid_ref, table_ref)
    for v in range(2):
        own_ref[v] = result[:WIN, v * 1024:(v + 1) * 1024]
        rows_ref[v] = result[WIN:, v * 1024:(v + 1) * 1024]


def edge_kernel(
    right_ref, corner_ref, table_ref, levels_ref, energy_ref, last_ref, inner_ref, inner_sums_ref,
    edge_ref, rows_ref, copies_ref,
    high_ref, low_ref, grid_ref,
):
    edge = by_rows(table_ref[BOTH, :], jnp.concatenate([right_ref[...], corner_ref[...]], axis=0))
    spread(back_by_stride([last_ref[...], edge]), high_ref, low_ref, 0)
    levels = levels_ref[INNER:, :]
    real, imag, power, sums = spectra(high_ref, low_ref, levels, table_ref)
    row = inner_sums_ref[...] + sums + packed(jnp.zeros((8, LANES), F32), jnp.zeros((8, LANES), F32), energy_ref[...])
    copies_ref[...] = jnp.broadcast_to(row[None], copies_ref.shape)
    for v, factor in enumerate((power, levels)):
        cols = adjoint_cols(real, imag, factor, table_ref)
        for c in range(2):
            for j, tile in enumerate(turned([cols[:, c * LANES:(c + 1) * LANES]])):
                place(grid_ref, c, tile, (v * 2 + j) * LANES)
    result = along_rows(grid_ref, table_ref)
    for v in range(2):
        mine = result[:, v * 2 * LANES:(v + 1) * 2 * LANES]
        edge_ref[v] = mine[:WIN]
        rows_ref[v, :, :7 * LANES] = inner_ref[v, :, :7 * LANES]
        rows_ref[v, :, 7 * LANES:8 * LANES] = inner_ref[v, :, 7 * LANES:] + mine[WIN:, :LANES]
        rows_ref[v, :, 8 * LANES:] = mine[WIN:, LANES:]


def vmem(count):
    return [pl.BlockSpec(memory_space=pltpu.VMEM)] * count


def local_part(*operands):
    return pl.pallas_call(
        local_kernel,
        out_shape=(
            pltpu.VMEM((1024, LANES), F32),
            pltpu.VMEM((128, 1024), F32),
            pltpu.VMEM((8, LANES), F32),
        ),
        in_specs=vmem(3),
        out_specs=tuple(vmem(3)),
        compiler_params=pltpu.CompilerParams(vmem_limit_bytes=24 * 1024 * 1024),
        cost_estimate=pl.CostEstimate(flops=10**8, bytes_accessed=3 * 10**6, transcendentals=0),
        name="local_part",
    )(*operands)


def inner_part(*operands):
    return pl.pallas_call(
        inner_kernel,
        out_shape=(
            pltpu.VMEM((2, WIN, 1024), F32),
            pltpu.VMEM((2, WIN, 1024), F32),
            pltpu.VMEM((128, LANES), F32),
            pltpu.VMEM((1, LANES), F32),
        ),
        in_specs=vmem(4),
        out_specs=tuple(vmem(4)),
        scratch_shapes=[
            pltpu.VMEM((INNER, 256), BF16),
            pltpu.VMEM((INNER, 256), BF16),
            pltpu.VMEM((256, 16 * LANES), BF16),
        ],
        compiler_params=pltpu.CompilerParams(vmem_limit_bytes=32 * 1024 * 1024),
        cost_estimate=pl.CostEstimate(flops=10**9, bytes_accessed=5 * 10**6, transcendentals=0),
        name="inner_part",
    )(*operands)


def edge_part(*operands):
    return pl.pallas_call(
        edge_kernel,
        out_shape=(
            pltpu.VMEM((2, WIN, 256), F32),
            pltpu.VMEM((2, WIN, 1152), F32),
            pltpu.VMEM((32, 1, LANES), F32),
        ),
        in_specs=vmem(8),
        out_specs=tuple(vmem(3)),
        scratch_shapes=[
            pltpu.VMEM((WIN, 256), BF16),
            pltpu.VMEM((WIN, 256), BF16),
            pltpu.VMEM((256, 4 * LANES), BF16),
        ],
        compiler_params=pltpu.CompilerParams(vmem_limit_bytes=16 * 1024 * 1024),
        cost_estimate=pl.CostEstimate(flops=10**8, bytes_accessed=2 * 10**6, transcendentals=0),
        name="edge_part",
    )(*operands)


def merge_kernel(own_ref, edge_ref, rows_ref, both_ref):
    both_ref[:, :, :7 * LANES] = own_ref[:, :, :7 * LANES] + rows_ref[:, :, :7 * LANES]
    last = slice(7 * LANES, 8 * LANES)
    both_ref[:, :, last] = own_ref[:, :, last] + edge_ref[:, :, :LANES] + rows_ref[:, :, last]


def merge_part(*operands):
    return pl.pallas_call(
        merge_kernel,
        out_shape=pltpu.VMEM((2, WIN, 1024), F32),
        in_specs=vmem(3),
        out_specs=vmem(1)[0],
        compiler_params=pltpu.CompilerParams(vmem_limit_bytes=16 * 1024 * 1024),
        cost_estimate=pl.CostEstimate(flops=10**6, bytes_accessed=MERGE_BYTES, transcendentals=0),
        name="merge_part",
    )(*operands)


def combine_kernel(both_ref, cols_ref, holo_ref, sums_ref, out_hbm, out_ref, sems):
    total = jnp.sum(sums_ref[...], axis=0, keepdims=True)
    energy = total[:, 2:3] / CELLS + 1e-5
    moment = total[:, 0:1] / energy - total[:, 1:2]
    inverse = 1.0 / energy
    slope = moment / (energy * energy * CELLS)
    copies = []
    for k in range(4):
        at = slice(k * 16, (k + 1) * 16)
        out_ref[at, :] = both_ref[0, at] * inverse - both_ref[1, at] - slope * holo_ref[at, :]
        out_ref[at, :LANES] += cols_ref[0, at] * inverse - cols_ref[1, at]
        copy = pltpu.make_async_copy(out_ref.at[pl.ds(k * 16, 16)], out_hbm.at[pl.ds(k * 16, 16)], sems.at[k])
        copy.start()
        copies.append(copy)
    for copy in copies:
        copy.wait()


def combine(*operands):
    return pl.pallas_call(
        combine_kernel,
        out_shape=pltpu.HBM((WIN, 1024), F32),
        in_specs=vmem(4),
        out_specs=pl.BlockSpec(memory_space=pl.ANY),
        scratch_shapes=[pltpu.VMEM((WIN, 1024), F32), pltpu.SemaphoreType.DMA((4,))],
        compiler_params=pltpu.CompilerParams(vmem_limit_bytes=16 * 1024 * 1024),
        cost_estimate=pl.CostEstimate(flops=10**6, bytes_accessed=2 * 10**6, transcendentals=0),
        name="combine",
    )(*operands)


def moved(block, rows, cols):
    row_size, col_size = lax.axis_size("row"), lax.axis_size("col")
    route = [
        (r * col_size + c, (r + rows) * col_size + c + cols)
        for r in range(row_size)
        for c in range(col_size)
        if 0 <= r + rows < row_size and 0 <= c + cols < col_size
    ]
    return lax.ppermute(block, AXES, route)


def shared(values, bits):
    masks = [0]
    for bit in bits:
        masks = masks + [mask ^ (1 << bit) for mask in masks]
    every = masks[-1]
    order = [mask ^ (LEAD & every) for mask in masks]
    groups = [[base | mask for mask in order] for base in range(512) if base & every == 0]
    copies = values
    if copies.ndim == 2:
        copies = jnp.broadcast_to(values[None], (len(masks), 1, LANES))
    return lax.all_to_all(copies, AXES, 0, 0, axis_index_groups=groups, tiled=True)


def per_device(hologram, target):
    holo = hologram.reshape(WIN, 1024)
    below = moved(holo, -1, 0)
    first = first_part(holo, zero_part())
    corner = moved(first, -1, -1)
    right = moved(first, 0, -1)
    levels, partial, energy = local_part(holo, target.reshape(32, 4096), TABLE)
    own, inner, last, sums = inner_part(below, TABLE, levels, partial)
    edge, rows, sums = edge_part(right, corner, TABLE, levels, energy, last, inner, sums)
    rows = moved(rows, 1, 0)
    cols = moved(edge[:, :, LANES:] + rows[:, :, 1024:], 0, 1)
    sums = jnp.sum(shared(sums, DEPTH_BITS), axis=0)
    both = merge_part(own, edge, rows)
    both, sums = lax.optimization_barrier((both, sums))
    sums = shared(sums, PLANE_BITS).reshape(-1, LANES)
    return combine(both, cols, holo, sums).reshape(2, STRIDE, 1024)


def solution(mesh):
    return jax.shard_map(
        per_device,
        mesh=mesh,
        in_specs=(P(None, "row", "col"), P("row", "col", None)),
        out_specs=P(None, "row", "col"),
        check_vma=False,
    )
```

time: 53.5 us -> 51.7 us (0.966)
  waiting for transfers between devices: 3.3 us -> 4.5 us
  starting transfers between devices: 32.1 us -> 31 us
  Pallas kernels: 6.38 us -> 5.33 us
  local copies, waits for them, and re-layouts: 0.77 us -> 0.02 us
    ppermute x5, starting transfers between devices: 19.4 us -> 15.2 us  [moved(): return lax.ppermute(block, AXES, route)]
    all_to_all x1, starting transfers between devices: 12.7 us -> 15.9 us  [shared(): lax.all_to_all(copies, AXES, 0, 0, axis_index_groups=groups, tiled=True)]
    pallas_call x3 -> x6, Pallas kernels: 6.33 us -> 5.28 us  [the longest x1 2.44 us: inner_part(): pl.pallas_call(inner_kernel, out_shape=(pltpu.VMEM((2, WIN, 1024), F32),...]
    all_to_all x1, waiting for transfers between devices: 1.42 us -> 2.29 us  [shared(): lax.all_to_all(copies, AXES, 0, 0, axis_index_groups=groups, tiled=True)]
    slice x1 -> x0, local copies, waits for them, and re-layouts: 0.76 us -> none  [per_device(): first = holo[:, :LANES]]
  transfers between devices with their start and end apart: 6 -> 6, of which waited for: 2 -> 2; matrix products, arithmetic and copies ran while one was open for 2% -> 0% of each run, Pallas kernels for 4% -> 6%
where the time goes in v3:
time: 51.7 us; the launch traced here: 51.2 us
  starting transfers between devices  31 us (60%)
  blocking collectives  10.1 us (20%)
  Pallas kernels  5.33 us (10%)
  waiting for transfers between devices  4.5 us (9%)
    all_to_all x1, starting transfers between devices, shared(): lax.all_to_all(copies, AXES, 0, 0, axis_index_groups=groups, tiled=True)  15.9 us
    ppermute x5, starting transfers between devices, moved(): return lax.ppermute(block, AXES, route)  15.2 us
    all_to_all x1, blocking collectives, shared(): lax.all_to_all(copies, AXES, 0, 0, axis_index_groups=groups, tiled=True)  10.1 us
    pallas_call x1, Pallas kernels, inner_part(): pl.pallas_call(inner_kernel, out_shape=(pltpu.VMEM((2, WIN, 1024), F32),...  2.44 us
    all_to_all x1, waiting for transfers between devices, shared(): lax.all_to_all(copies, AXES, 0, 0, axis_index_groups=groups, tiled=True)  2.29 us
    ppermute x5, waiting for transfers between devices, moved(): return lax.ppermute(block, AXES, route)  2.21 us
    pallas_call x1, Pallas kernels, edge_part(): pl.pallas_call(edge_kernel, out_shape=(pltpu.VMEM((2, WIN, 256), F32), pl...  1.52 us
  transfers between devices with their start and end apart: 6, of which 2 were waited for; matrix products, arithmetic and copies ran while one was open for 0% of the time, Pallas kernels for 6%

profile of v3, /device:TPU:1, one launch (start us, length us, event | category | flops | bytes accessed | tf_op | source)
XLA Modules:
  0.0 51.2 jit_solution(8884377625673568758)
XLA Ops:
  0.0 0.0 copy-start.1
  0.0 8.9 %collective-permute-start = (f32[64,1024]{1,0:T(8,128)}, f32[64,1024]{1,0:T(8,128)S(1)}, u32[]{:S(2)}, u32[]{:S(2)}) collective-permute-start(f32[64,1024]{1,0:T(8,128)} %bitcast.6), channel_id=1, source_target_pairs={{32,0},{33,1},{34,2},{35,3},{36,4},{37,5},{38,6},{39,7},{40,8},{41... | collective-permute-start | bytes 786440 | tf_op jit(solution)/shard_map/ppermute | solution.py:404
  8.9 0.0 copy-start
  8.9 0.0 copy-done.1
  8.9 0.0 copy-start.2
  9.0 1.4 %collective-permute-start.1 = (f32[64,128]{1,0:T(8,128)S(1)}, f32[64,128]{1,0:T(8,128)S(1)}, u32[]{:S(2)}, u32[]{:S(2)}) collective-permute-start(f32[64,128]{1,0:T(8,128)S(1)} %first_part.1), channel_id=1, source_target_pairs={{1,0},{2,1},{3,2},{4,3},{5,4},{6,5},{7,6},{8,7},{9,8},{10,9},{11,1... | collective-permute-start | bytes 98312 | tf_op jit(solution)/shard_map/ppermute | solution.py:404
  10.4 1.3 %collective-permute-start.2 = (f32[64,128]{1,0:T(8,128)S(1)}, f32[64,128]{1,0:T(8,128)S(1)}, u32[]{:S(2)}, u32[]{:S(2)}) collective-permute-start(f32[64,128]{1,0:T(8,128)S(1)} %first_part.1), channel_id=1, source_target_pairs={{33,0},{34,1},{35,2},{36,3},{37,4},{38,5},{39,6},{40,7},{41,8},{42... | collective-permute-start | bytes 98312 | tf_op jit(solution)/shard_map/ppermute | solution.py:404
  11.7 0.0 copy-done
  11.7 0.0 copy-done.2
  11.7 0.4 local_part.1
  12.2 0.0 collective-permute-done.below_ref
  12.2 2.4 %inner_part.1 = (f32[2,64,1024]{2,1,0:T(8,128)S(1)}, f32[2,64,1024]{2,1,0:T(8,128)S(1)}, f32[128,128]{1,0:T(8,128)S(1)}, f32[1,128]{1,0:T(1,128)S(1)}) custom-call(f32[64,1024]{1,0:T(8,128)S(1)} %collective-permute-done.below_ref, bf16[1536,256]{1,0:T(8,128)(2,1)S(1)} %copy-done, f32[1024,128]{1,0:T(8,128)S(1)} %get-tuple-element.17.levels_ref, ...), custom_call_target="tpu_custom_call" | custom-call | flops 1000000000 | bytes 5000000 | tf_op jit(solution)/shard_map/inner_part/pallas_call | solution.py:305
  14.6 0.0 collective-permute-done.1.right_ref
  14.7 2.2 %collective-permute-done.2.corner_ref = f32[64,128]{1,0:T(8,128)S(1)} collective-permute-done((f32[64,128]{1,0:T(8,128)S(1)}, f32[64,128]{1,0:T(8,128)S(1)}, u32[]{:S(2)}, u32[]{:S(2)}) %collective-permute-start.2) | collective-permute-done | bytes 32800 | tf_op jit(solution)/shard_map/ppermute | solution.py:404
  16.9 1.5 %edge_part.1 = (f32[2,64,256]{2,1,0:T(8,128)S(1)}, f32[2,64,1152]{2,1,0:T(8,128)S(1)}, f32[32,1,128]{2,1,0:T(1,128)}) custom-call(f32[64,128]{1,0:T(8,128)S(1)} %collective-permute-done.1.right_ref, f32[64,128]{1,0:T(8,128)S(1)} %collective-permute-done.2.corner_ref, bf16[1536,256]{1,0:T(8,128)(2,1)S(1)} %copy-done, ...), custom_call_target="tpu_custom_call" | custom-call | flops 100000000 | bytes 2000000 | tf_op jit(solution)/shard_map/edge_part/pallas_call | solution.py:327
  18.4 1.9 %collective-permute-start.3 = (f32[2,64,1152]{2,1,0:T(8,128)S(1)}, f32[2,64,1152]{2,1,0:T(8,128)S(1)}, u32[]{:S(2)}, u32[]{:S(2)}) collective-permute-start(f32[2,64,1152]{2,1,0:T(8,128)S(1)} %get-tuple-element.25), channel_id=1, source_target_pairs={{0,32},{1,33},{2,34},{3,35},{4,36},{5,37},{6,38},{7,39},{8,40},{9,... | collective-permute-start | bytes 1769480 | tf_op jit(solution)/shard_map/ppermute | solution.py:404
  20.3 15.9 %all-to-all-start = ((f32[32,1,128]{2,1,0:T(1,128)}), f32[32,1,128]{2,1,0:T(1,128)S(1)}, u32[]{:S(2)}, u32[]{:S(2)}) async-start(f32[32,1,128]{2,1,0:T(1,128)} %get-tuple-element.26), calls=%async_computation | async-start | bytes 32768 | tf_op jit(solution)/shard_map/all_to_all | solution.py:417
  36.2 0.0 collective-permute-done.3.rows_ref
  36.2 1.6 %collective-permute-start.4 = (f32[2,64,128]{2,1,0:T(8,128)S(1)}, f32[2,64,128]{2,1,0:T(8,128)S(1)}, u32[]{:S(2)}, u32[]{:S(2)}) collective-permute-start(f32[2,64,128]{2,1,0:T(8,128)S(1)} %slice_add_fusion), channel_id=1, source_target_pairs={{0,1},{1,2},{2,3},{3,4},{4,5},{5,6},{6,7},{7,8},{8,9},{9,10},{10,1... | collective-permute-start | bytes 196616 | tf_op jit(solution)/shard_map/ppermute | solution.py:404
  37.8 2.3 %all-to-all-done = f32[32,1,128]{2,1,0:T(1,128)S(1)} async-done(((f32[32,1,128]{2,1,0:T(1,128)}), f32[32,1,128]{2,1,0:T(1,128)S(1)}, u32[]{:S(2)}, u32[]{:S(2)}) %all-to-all-start) | async-done | bytes 16416 | tf_op jit(solution)/shard_map/all_to_all | solution.py:417
  40.1 0.1 reduce_sum.11
  40.2 0.1 merge_part.1.both_ref
  40.3 10.1 %all_to_all.10 = f32[16,1,128]{2,1,0:T(1,128)S(1)} all-to-all(f32[16,1,128]{2,1,0:T(1,128)S(1)} %broadcast_in_dim.9), channel_id=1, replica_groups={{321,320,257,256,449,448,385,384,65,64,1,0,193,192,129,128},{323,322,25..., dimensions={0} | all-to-all | bytes 16384 | tf_op jit(solution)/shard_map/all_to_all | solution.py:417
  50.3 0.0 collective-permute-done.4.cols_ref
  50.3 0.9 %combine.1 = f32[64,1024]{1,0:T(8,128)} custom-call(f32[2,64,1024]{2,1,0:T(8,128)S(1)} %merge_part.1.both_ref, f32[2,64,128]{2,1,0:T(8,128)S(1)} %collective-permute-done.4.cols_ref, f32[64,1024]{1,0:T(8,128)S(1)} %bitcast.9, f32[16,128]{1,0:T(8,128)S(1)} %bitcast.11), custom_call_target="tpu_custom_call" | custom-call | flops 1000000 | bytes 2000000 | tf_op jit(solution)/shard_map/combine/pallas_call | solution.py:384
  (4 shorter events, 0.0 us)
Async XLA Ops:
  0.0 8.9 %copy-start.1 = (f32[2,32,1024]{2,1,0:T(8,128)S(1)}, f32[2,32,1024]{2,1,0:T(8,128)}, u32[]{:S(2)}) copy-start(f32[2,32,1024]{2,1,0:T(8,128)} %param.3) | copy-start | bytes 786436
  0.0 12.2 %collective-permute-start = (f32[64,1024]{1,0:T(8,128)}, f32[64,1024]{1,0:T(8,128)S(1)}, u32[]{:S(2)}, u32[]{:S(2)}) collective-permute-start(f32[64,1024]{1,0:T(8,128)} %bitcast.6), channel_id=1, source_target_pairs={{32,0},{33,1},{34,2},{35,3},{36,4},{37,5},{38,6},{39,7},{40,8},{41... | collective-permute-start | bytes 786440 | tf_op jit(solution)/shard_map/ppermute | solution.py:404
  8.9 2.8 %copy-start = (bf16[1536,256]{1,0:T(8,128)(2,1)S(1)}, bf16[1536,256]{1,0:T(8,128)(2,1)}, u32[]{:S(2)}) copy-start(bf16[1536,256]{1,0:T(8,128)(2,1)} %constant.4.clone.table_ref) | copy-start | bytes 2359300
  8.9 2.8 %copy-start.2 = (bf16[1,32,4096]{2,1,0:T(8,128)(2,1)S(1)}, bf16[1,32,4096]{2,1,0:T(8,128)(2,1)}, u32[]{:S(2)}) copy-start(bf16[1,32,4096]{2,1,0:T(8,128)(2,1)} %param.4) | copy-start | bytes 786436
  9.0 5.7 %collective-permute-start.1 = (f32[64,128]{1,0:T(8,128)S(1)}, f32[64,128]{1,0:T(8,128)S(1)}, u32[]{:S(2)}, u32[]{:S(2)}) collective-permute-start(f32[64,128]{1,0:T(8,128)S(1)} %first_part.1), channel_id=1, source_target_pairs={{1,0},{2,1},{3,2},{4,3},{5,4},{6,5},{7,6},{8,7},{9,8},{10,9},{11,1... | collective-permute-start | bytes 98312 | tf_op jit(solution)/shard_map/ppermute | solution.py:404
  10.4 6.4 %collective-permute-start.2 = (f32[64,128]{1,0:T(8,128)S(1)}, f32[64,128]{1,0:T(8,128)S(1)}, u32[]{:S(2)}, u32[]{:S(2)}) collective-permute-start(f32[64,128]{1,0:T(8,128)S(1)} %first_part.1), channel_id=1, source_target_pairs={{33,0},{34,1},{35,2},{36,3},{37,4},{38,5},{39,6},{40,7},{41,8},{42... | collective-permute-start | bytes 98312 | tf_op jit(solution)/shard_map/ppermute | solution.py:404
  18.4 17.8 %collective-permute-start.3 = (f32[2,64,1152]{2,1,0:T(8,128)S(1)}, f32[2,64,1152]{2,1,0:T(8,128)S(1)}, u32[]{:S(2)}, u32[]{:S(2)}) collective-permute-start(f32[2,64,1152]{2,1,0:T(8,128)S(1)} %get-tuple-element.25), channel_id=1, source_target_pairs={{0,32},{1,33},{2,34},{3,35},{4,36},{5,37},{6,38},{7,39},{8,40},{9,... | collective-permute-start | bytes 1769480 | tf_op jit(solution)/shard_map/ppermute | solution.py:404
  20.3 19.8 %all-to-all-start = ((f32[32,1,128]{2,1,0:T(1,128)}), f32[32,1,128]{2,1,0:T(1,128)S(1)}, u32[]{:S(2)}, u32[]{:S(2)}) async-start(f32[32,1,128]{2,1,0:T(1,128)} %get-tuple-element.26), calls=%async_computation | async-start | bytes 32768 | tf_op jit(solution)/shard_map/all_to_all | solution.py:417
  36.2 14.1 %collective-permute-start.4 = (f32[2,64,128]{2,1,0:T(8,128)S(1)}, f32[2,64,128]{2,1,0:T(8,128)S(1)}, u32[]{:S(2)}, u32[]{:S(2)}) collective-permute-start(f32[2,64,128]{2,1,0:T(8,128)S(1)} %slice_add_fusion), channel_id=1, source_target_pairs={{0,1},{1,2},{2,3},{3,4},{4,5},{5,6},{6,7},{7,8},{8,9},{9,10},{10,1... | collective-permute-start | bytes 196616 | tf_op jit(solution)/shard_map/ppermute | solution.py:404

commit v4 on v3

--- a/solution.py
+++ b/solution.py
@@ -13,7 +13,7 @@
 AXES = ("row", "col")
 DEPTH_BITS = (5, 1, 2, 3, 4)
 PLANE_BITS = (0, 6, 7, 8)
-LEAD = 11 * 32 + 21
+LEAD = 11 * 32 + 20
 BF16 = jnp.bfloat16
 F32 = jnp.float32
 CELLS = 512.0 * 32768.0
@@ -208,11 +208,11 @@
     return [jnp.where(lane < LANES - STRIDE, here, after) for here, after in zip(ahead[:-1], ahead[1:])]
 
 
-def spectra(high_ref, low_ref, levels, table_ref):
+def spectra(high_ref, low_ref, levels, table_ref, *terms):
     spectrum = along_cols(high_ref[...], low_ref[...], table_ref)
     real, imag = spectrum[:, :LANES], spectrum[:, LANES:]
     power = real * real + imag * imag
-    return real, imag, power, packed(power * power, levels * power)
+    return real, imag, power, packed(power * power, levels * power, *terms)
 
 
 def adjoint_cols(real, imag, factor, table_ref):
@@ -226,15 +226,15 @@
     grid_ref[128 + c * WIN:128 + (c + 1) * WIN, at:at + LANES] = low
 
 
-def along_rows(grid_ref, table_ref):
-    result = mul(table_ref[BACK, :], grid_ref[...])
+def along_rows(grid, table_ref):
+    result = mul(table_ref[BACK, :], grid)
     return result[:128] + result[128:]
 
 
 def inner_kernel(
-    below_ref, table_ref, levels_ref, partial_ref,
-    own_ref, rows_ref, last_ref, sums_ref,
-    high_ref, low_ref, grid_ref,
+    below_ref, table_ref, levels_ref, partial_ref, energy_ref,
+    grid_ref, last_ref, seam_ref, sums_ref,
+    high_ref, low_ref,
 ):
     main = partial_ref[...] + by_rows(table_ref[NEXT, :128], below_ref[...])
     tiles = [main[:, j * LANES:(j + 1) * LANES] for j in range(8)]
@@ -242,43 +242,58 @@
     spread(tiles, high_ref, low_ref, 0)
     spread(back_by_stride(tiles), high_ref, low_ref, 8)
     levels = levels_ref[:INNER, :]
-    real, imag, power, sums_ref[...] = spectra(high_ref, low_ref, levels, table_ref)
+    real, imag, power, sums_ref[...] = spectra(high_ref, low_ref, levels, table_ref, energy_ref[...])
     for v, factor in enumerate((power, levels)):
         cols = adjoint_cols(real, imag, factor, table_ref)
         for c in range(2):
             lanes = slice(c * LANES, (c + 1) * LANES)
             odd = turned([cols[(8 + j) * WIN:(9 + j) * WIN, lanes] for j in range(7)])
-            for j in range(8):
-                place(grid_ref, c, odd[j] + cols[j * WIN:(j + 1) * WIN, lanes], (v * 8 + j) * LANES)
-    result = along_rows(grid_ref, table_ref)
-    for v in range(2):
-        own_ref[v] = result[:WIN, v * 1024:(v + 1) * 1024]
-        rows_ref[v] = result[WIN:, v * 1024:(v + 1) * 1024]
+            for j in range(7):
+                place(grid_ref, c, odd[j] + cols[j * WIN:(j + 1) * WIN, lanes], (v * 7 + j) * LANES)
+            seam_ref[v, c * WIN:(c + 1) * WIN] = odd[7] + cols[7 * WIN:8 * WIN, lanes]
 
 
 def edge_kernel(
-    right_ref, corner_ref, table_ref, levels_ref, energy_ref, last_ref, inner_ref, inner_sums_ref,
-    edge_ref, rows_ref, copies_ref,
-    high_ref, low_ref, grid_ref,
+    right_ref, corner_ref, table_ref, levels_ref, grid_ref, last_ref, seam_ref, inner_sums_ref,
+    own_ref, rows_ref, tail_ref, sums_hbm,
+    high_ref, low_ref, edge_ref, copies_ref, fields_ref, sem,
 ):
-    edge = by_rows(table_ref[BOTH, :], jnp.concatenate([right_ref[...], corner_ref[...]], axis=0))
-    spread(back_by_stride([last_ref[...], edge]), high_ref, low_ref, 0)
+    copy = pltpu.make_async_copy(copies_ref, sums_hbm, sem)
     levels = levels_ref[INNER:, :]
-    real, imag, power, sums = spectra(high_ref, low_ref, levels, table_ref)
-    row = inner_sums_ref[...] + sums + packed(jnp.zeros((8, LANES), F32), jnp.zeros((8, LANES), F32), energy_ref[...])
-    copies_ref[...] = jnp.broadcast_to(row[None], copies_ref.shape)
-    for v, factor in enumerate((power, levels)):
-        cols = adjoint_cols(real, imag, factor, table_ref)
-        for c in range(2):
-            for j, tile in enumerate(turned([cols[:, c * LANES:(c + 1) * LANES]])):
-                place(grid_ref, c, tile, (v * 2 + j) * LANES)
-    result = along_rows(grid_ref, table_ref)
-    for v in range(2):
-        mine = result[:, v * 2 * LANES:(v + 1) * 2 * LANES]
-        edge_ref[v] = mine[:WIN]
-        rows_ref[v, :, :7 * LANES] = inner_ref[v, :, :7 * LANES]
-        rows_ref[v, :, 7 * LANES:8 * LANES] = inner_ref[v, :, 7 * LANES:] + mine[WIN:, :LANES]
-        rows_ref[v, :, 8 * LANES:] = mine[WIN:, LANES:]
+
+    @pl.when(pl.program_id(0) == 0)
+    def _():
+        edge = by_rows(table_ref[BOTH, :], jnp.concatenate([right_ref[...], corner_ref[...]], axis=0))
+        spread(back_by_stride([last_ref[...], edge]), high_ref, low_ref, 0)
+        real, imag, power, sums = spectra(high_ref, low_ref, levels, table_ref)
+        fields_ref[0], fields_ref[1], fields_ref[2] = real, imag, power
+        row = inner_sums_ref[...] + sums
+        copies_ref[...] = jnp.broadcast_to(row[None], copies_ref.shape)
+        copy.start()
+
+    @pl.when(pl.program_id(0) == 1)
+    def _():
+        real, imag, power = fields_ref[0], fields_ref[1], fields_ref[2]
+        for v, factor in enumerate((power, levels)):
+            cols = adjoint_cols(real, imag, factor, table_ref)
+            for c in range(2):
+                seam, tail = turned([cols[:, c * LANES:(c + 1) * LANES]])
+                place(edge_ref, c, seam + seam_ref[v, c * WIN:(c + 1) * WIN], v * 2 * LANES)
+                place(edge_ref, c, tail, (v * 2 + 1) * LANES)
+        result = along_rows(grid_ref[...], table_ref)
+        for v in range(2):
+            lanes = slice(v * 7 * LANES, (v + 1) * 7 * LANES)
+            own_ref[v, :, :7 * LANES] = result[:WIN, lanes]
+            rows_ref[v, :, :7 * LANES] = result[WIN:, lanes]
+        result = along_rows(edge_ref[...], table_ref)
+        for v in range(2):
+            seam = result[:, v * 2 * LANES:(v * 2 + 1) * LANES]
+            tail = result[:, (v * 2 + 1) * LANES:(v * 2 + 2) * LANES]
+            own_ref[v, :, 7 * LANES:] = seam[:WIN]
+            tail_ref[v] = tail[:WIN]
+            rows_ref[v, :, 7 * LANES:8 * LANES] = seam[WIN:]
+            rows_ref[v, :, 8 * LANES:] = tail[WIN:]
+        copy.wait()
 
 
 def vmem(count):
@@ -305,17 +320,16 @@
     return pl.pallas_call(
         inner_kernel,
         out_shape=(
-            pltpu.VMEM((2, WIN, 1024), F32),
-            pltpu.VMEM((2, WIN, 1024), F32),
+            pltpu.VMEM((256, 14 * LANES), BF16),
             pltpu.VMEM((128, LANES), F32),
+            pltpu.VMEM((2, 128, LANES), F32),
             pltpu.VMEM((1, LANES), F32),
         ),
-        in_specs=vmem(4),
+        in_specs=vmem(5),
         out_specs=tuple(vmem(4)),
         scratch_shapes=[
             pltpu.VMEM((INNER, 256), BF16),
             pltpu.VMEM((INNER, 256), BF16),
-            pltpu.VMEM((256, 16 * LANES), BF16),
         ],
         compiler_params=pltpu.CompilerParams(vmem_limit_bytes=32 * 1024 * 1024),
         cost_estimate=pl.CostEstimate(flops=10**9, bytes_accessed=5 * 10**6, transcendentals=0),
@@ -327,16 +341,21 @@
     return pl.pallas_call(
         edge_kernel,
         out_shape=(
-            pltpu.VMEM((2, WIN, 256), F32),
+            pltpu.VMEM((2, WIN, 1024), F32),
             pltpu.VMEM((2, WIN, 1152), F32),
-            pltpu.VMEM((32, 1, LANES), F32),
+            pltpu.VMEM((2, WIN, LANES), F32),
+            pltpu.HBM((32, 1, LANES), F32),
         ),
+        grid=(2,),
         in_specs=vmem(8),
-        out_specs=tuple(vmem(3)),
+        out_specs=tuple(vmem(3)) + (pl.BlockSpec(memory_space=pl.ANY),),
         scratch_shapes=[
             pltpu.VMEM((WIN, 256), BF16),
             pltpu.VMEM((WIN, 256), BF16),
             pltpu.VMEM((256, 4 * LANES), BF16),
+            pltpu.VMEM((32, 1, LANES), F32),
+            pltpu.VMEM((3, WIN, LANES), F32),
+            pltpu.SemaphoreType.DMA,
         ],
         compiler_params=pltpu.CompilerParams(vmem_limit_bytes=16 * 1024 * 1024),
         cost_estimate=pl.CostEstimate(flops=10**8, bytes_accessed=2 * 10**6, transcendentals=0),
@@ -344,17 +363,15 @@
     )(*operands)
 
 
-def merge_kernel(own_ref, edge_ref, rows_ref, both_ref):
-    both_ref[:, :, :7 * LANES] = own_ref[:, :, :7 * LANES] + rows_ref[:, :, :7 * LANES]
-    last = slice(7 * LANES, 8 * LANES)
-    both_ref[:, :, last] = own_ref[:, :, last] + edge_ref[:, :, :LANES] + rows_ref[:, :, last]
+def merge_kernel(own_ref, rows_ref, both_ref):
+    both_ref[...] = own_ref[...] + rows_ref[:, :, :1024]
 
 
 def merge_part(*operands):
     return pl.pallas_call(
         merge_kernel,
         out_shape=pltpu.VMEM((2, WIN, 1024), F32),
-        in_specs=vmem(3),
+        in_specs=vmem(2),
         out_specs=vmem(1)[0],
         compiler_params=pltpu.CompilerParams(vmem_limit_bytes=16 * 1024 * 1024),
         cost_estimate=pl.CostEstimate(flops=10**6, bytes_accessed=MERGE_BYTES, transcendentals=0),
@@ -424,12 +441,12 @@
     corner = moved(first, -1, -1)
     right = moved(first, 0, -1)
     levels, partial, energy = local_part(holo, target.reshape(32, 4096), TABLE)
-    own, inner, last, sums = inner_part(below, TABLE, levels, partial)
-    edge, rows, sums = edge_part(right, corner, TABLE, levels, energy, last, inner, sums)
+    inner = inner_part(below, TABLE, levels, partial, energy)
+    own, rows, tail, sums = edge_part(right, corner, TABLE, levels, *inner)
     rows = moved(rows, 1, 0)
-    cols = moved(edge[:, :, LANES:] + rows[:, :, 1024:], 0, 1)
+    cols = moved(tail + rows[:, :, 1024:], 0, 1)
     sums = jnp.sum(shared(sums, DEPTH_BITS), axis=0)
-    both = merge_part(own, edge, rows)
+    both = merge_part(own, rows)
     both, sums = lax.optimization_barrier((both, sums))
     sums = shared(sums, PLANE_BITS).reshape(-1, LANES)
     return combine(both, cols, holo, sums).reshape(2, STRIDE, 1024)

time: 51.7 us -> 50.6 us (0.979)
  waiting for transfers between devices: 4.5 us -> 3.04 us
  starting transfers between devices: 31 us -> 32.4 us
  Pallas kernels: 5.33 us -> 4.46 us
    ppermute x5, starting transfers between devices: 15.2 us -> 19.7 us  [moved(): return lax.ppermute(block, AXES, route)]
    all_to_all x1, starting transfers between devices: 15.9 us -> 12.7 us  [shared(): lax.all_to_all(copies, AXES, 0, 0, axis_index_groups=groups, tiled=True)]
    pallas_call x2, Pallas kernels: 3.96 us -> 3.09 us  [the longest x1 1.76 us: inner_part(): pl.pallas_call(inner_kernel, out_shape=(pltpu.VMEM((256, 14 * LANES), BF1...]
    all_to_all x1, waiting for transfers between devices: 2.29 us -> 1.43 us  [shared(): lax.all_to_all(copies, AXES, 0, 0, axis_index_groups=groups, tiled=True)]
    ppermute x5, waiting for transfers between devices: 2.21 us -> 1.61 us  [moved(): return lax.ppermute(block, AXES, route)]
  transfers between devices with their start and end apart: 6 -> 6, of which waited for: 2 -> 2; matrix products, arithmetic and copies ran while one was open for 0% -> 0% of each run, Pallas kernels for 6% -> 5%
where the time goes in v4:
time: 50.6 us; the launch traced here: 50 us
  starting transfers between devices  32.4 us (64%)
  blocking collectives  9.84 us (19%)
  Pallas kernels  4.46 us (9%)
  waiting for transfers between devices  3.04 us (6%)
    ppermute x5, starting transfers between devices, moved(): return lax.ppermute(block, AXES, route)  19.7 us
    all_to_all x1, starting transfers between devices, shared(): lax.all_to_all(copies, AXES, 0, 0, axis_index_groups=groups, tiled=True)  12.7 us
    all_to_all x1, blocking collectives, shared(): lax.all_to_all(copies, AXES, 0, 0, axis_index_groups=groups, tiled=True)  9.84 us
    pallas_call x1, Pallas kernels, inner_part(): pl.pallas_call(inner_kernel, out_shape=(pltpu.VMEM((256, 14 * LANES), BF1...  1.76 us
    ppermute x5, waiting for transfers between devices, moved(): return lax.ppermute(block, AXES, route)  1.61 us
    all_to_all x1, waiting for transfers between devices, shared(): lax.all_to_all(copies, AXES, 0, 0, axis_index_groups=groups, tiled=True)  1.43 us
    pallas_call x1, Pallas kernels, edge_part(): pl.pallas_call(edge_kernel, out_shape=(pltpu.VMEM((2, WIN, 1024), F32), p...  1.33 us
  transfers between devices with their start and end apart: 6, of which 2 were waited for; matrix products, arithmetic and copies ran while one was open for 0% of the time, Pallas kernels for 5%

profile of v4, /device:TPU:1, one launch (start us, length us, event | category | flops | bytes accessed | tf_op | source)
XLA Modules:
  0.0 50.0 jit_solution(6659243294468261780)
XLA Ops:
  0.0 0.0 copy-start.1
  0.0 8.9 %collective-permute-start.2 = (f32[64,1024]{1,0:T(8,128)}, f32[64,1024]{1,0:T(8,128)S(1)}, u32[]{:S(2)}, u32[]{:S(2)}) collective-permute-start(f32[64,1024]{1,0:T(8,128)} %bitcast.6), channel_id=1, source_target_pairs={{32,0},{33,1},{34,2},{35,3},{36,4},{37,5},{38,6},{39,7},{40,8},{41... | collective-permute-start | bytes 786440 | tf_op jit(solution)/shard_map/ppermute | solution.py:421
  8.9 0.0 copy-start
  8.9 0.0 copy-done.1
  8.9 0.0 copy-start.2
  9.0 1.4 %collective-permute-start.1 = (f32[64,128]{1,0:T(8,128)S(1)}, f32[64,128]{1,0:T(8,128)S(1)}, u32[]{:S(2)}, u32[]{:S(2)}) collective-permute-start(f32[64,128]{1,0:T(8,128)S(1)} %first_part.1), channel_id=1, source_target_pairs={{33,0},{34,1},{35,2},{36,3},{37,4},{38,5},{39,6},{40,7},{41,8},{42... | collective-permute-start | bytes 98312 | tf_op jit(solution)/shard_map/ppermute | solution.py:421
  10.4 1.3 %collective-permute-start = (f32[64,128]{1,0:T(8,128)S(1)}, f32[64,128]{1,0:T(8,128)S(1)}, u32[]{:S(2)}, u32[]{:S(2)}) collective-permute-start(f32[64,128]{1,0:T(8,128)S(1)} %first_part.1), channel_id=1, source_target_pairs={{1,0},{2,1},{3,2},{4,3},{5,4},{6,5},{7,6},{8,7},{9,8},{10,9},{11,1... | collective-permute-start | bytes 98312 | tf_op jit(solution)/shard_map/ppermute | solution.py:421
  11.7 0.0 copy-done
  11.7 0.0 copy-done.2
  11.7 0.4 local_part.1
  12.2 0.0 collective-permute-done.2.below_ref
  12.2 1.8 %inner_part.1 = (bf16[256,1792]{1,0:T(8,128)(2,1)S(1)}, f32[128,128]{1,0:T(8,128)S(1)}, f32[2,128,128]{2,1,0:T(8,128)S(1)}, f32[1,128]{1,0:T(1,128)S(1)}) custom-call(f32[64,1024]{1,0:T(8,128)S(1)} %collective-permute-done.2.below_ref, bf16[1536,256]{1,0:T(8,128)(2,1)S(1)} %copy-done, f32[1024,128]{1,0:T(8,128)S(1)} %get-tuple-element.18.levels_ref, ...), custom_call_target="tpu_custom_call" | custom-call | flops 1000000000 | bytes 5000000 | tf_op jit(solution)/shard_map/inner_part/pallas_call | solution.py:320
  14.0 1.6 %collective-permute-done.1.corner_ref = f32[64,128]{1,0:T(8,128)S(1)} collective-permute-done((f32[64,128]{1,0:T(8,128)S(1)}, f32[64,128]{1,0:T(8,128)S(1)}, u32[]{:S(2)}, u32[]{:S(2)}) %collective-permute-start.1) | collective-permute-done | bytes 32800 | tf_op jit(solution)/shard_map/ppermute | solution.py:421
  15.6 0.0 collective-permute-done.right_ref
  15.6 1.3 %edge_part.1 = (f32[2,64,1024]{2,1,0:T(8,128)S(1)}, f32[2,64,1152]{2,1,0:T(8,128)S(1)}, f32[2,64,128]{2,1,0:T(8,128)S(1)}, f32[32,1,128]{2,1,0:T(1,128)}) custom-call(f32[64,128]{1,0:T(8,128)S(1)} %collective-permute-done.right_ref, f32[64,128]{1,0:T(8,128)S(1)} %collective-permute-done.1.corner_ref, bf16[1536,256]{1,0:T(8,128)(2,1)S(1)} %copy-done, ...), custom_call_target="tpu_custom_call" | custom-call | flops 100000000 | bytes 2000000 | tf_op jit(solution)/shard_map/edge_part/pallas_call | solution.py:341
  16.9 5.6 %collective-permute-start.3 = (f32[2,64,1152]{2,1,0:T(8,128)S(1)}, f32[2,64,1152]{2,1,0:T(8,128)S(1)}, u32[]{:S(2)}, u32[]{:S(2)}) collective-permute-start(f32[2,64,1152]{2,1,0:T(8,128)S(1)} %get-tuple-element.26), channel_id=1, source_target_pairs={{0,32},{1,33},{2,34},{3,35},{4,36},{5,37},{6,38},{7,39},{8,40},{9,... | collective-permute-start | bytes 1769480 | tf_op jit(solution)/shard_map/ppermute | solution.py:421
  22.5 12.7 %all-to-all-start = ((f32[32,1,128]{2,1,0:T(1,128)}), f32[32,1,128]{2,1,0:T(1,128)S(1)}, u32[]{:S(2)}, u32[]{:S(2)}) async-start(f32[32,1,128]{2,1,0:T(1,128)} %get-tuple-element.27), calls=%async_computation | async-start | bytes 32768 | tf_op jit(solution)/shard_map/all_to_all | solution.py:434
  35.2 0.0 collective-permute-done.3.rows_ref
  35.2 2.5 %collective-permute-start.4 = (f32[2,64,128]{2,1,0:T(8,128)S(1)}, f32[2,64,128]{2,1,0:T(8,128)S(1)}, u32[]{:S(2)}, u32[]{:S(2)}) collective-permute-start(f32[2,64,128]{2,1,0:T(8,128)S(1)} %slice_add_fusion), channel_id=1, source_target_pairs={{0,1},{1,2},{2,3},{3,4},{4,5},{5,6},{6,7},{7,8},{8,9},{9,10},{10,1... | collective-permute-start | bytes 196616 | tf_op jit(solution)/shard_map/ppermute | solution.py:421
  37.7 1.4 %all-to-all-done = f32[32,1,128]{2,1,0:T(1,128)S(1)} async-done(((f32[32,1,128]{2,1,0:T(1,128)}), f32[32,1,128]{2,1,0:T(1,128)S(1)}, u32[]{:S(2)}, u32[]{:S(2)}) %all-to-all-start) | async-done | bytes 16416 | tf_op jit(solution)/shard_map/all_to_all | solution.py:434
  39.1 0.1 reduce_sum.11
  39.2 0.1 merge_part.1.both_ref
  39.3 9.8 %all_to_all.10 = f32[16,1,128]{2,1,0:T(1,128)S(1)} all-to-all(f32[16,1,128]{2,1,0:T(1,128)S(1)} %broadcast_in_dim.9), channel_id=1, replica_groups={{320,321,256,257,448,449,384,385,64,65,0,1,192,193,128,129},{322,323,25..., dimensions={0} | all-to-all | bytes 16384 | tf_op jit(solution)/shard_map/all_to_all | solution.py:434
  49.1 0.0 collective-permute-done.4.cols_ref
  49.1 0.9 %combine.1 = f32[64,1024]{1,0:T(8,128)} custom-call(f32[2,64,1024]{2,1,0:T(8,128)S(1)} %merge_part.1.both_ref, f32[2,64,128]{2,1,0:T(8,128)S(1)} %collective-permute-done.4.cols_ref, f32[64,1024]{1,0:T(8,128)S(1)} %bitcast.9, f32[16,128]{1,0:T(8,128)S(1)} %bitcast.11), custom_call_target="tpu_custom_call" | custom-call | flops 1000000 | bytes 2000000 | tf_op jit(solution)/shard_map/combine/pallas_call | solution.py:401
  (4 shorter events, 0.0 us)
Async XLA Ops:
  0.0 8.9 %copy-start.1 = (f32[2,32,1024]{2,1,0:T(8,128)S(1)}, f32[2,32,1024]{2,1,0:T(8,128)}, u32[]{:S(2)}) copy-start(f32[2,32,1024]{2,1,0:T(8,128)} %param.3) | copy-start | bytes 786436
  0.0 12.2 %collective-permute-start.2 = (f32[64,1024]{1,0:T(8,128)}, f32[64,1024]{1,0:T(8,128)S(1)}, u32[]{:S(2)}, u32[]{:S(2)}) collective-permute-start(f32[64,1024]{1,0:T(8,128)} %bitcast.6), channel_id=1, source_target_pairs={{32,0},{33,1},{34,2},{35,3},{36,4},{37,5},{38,6},{39,7},{40,8},{41... | collective-permute-start | bytes 786440 | tf_op jit(solution)/shard_map/ppermute | solution.py:421
  8.9 2.8 %copy-start = (bf16[1536,256]{1,0:T(8,128)(2,1)S(1)}, bf16[1536,256]{1,0:T(8,128)(2,1)}, u32[]{:S(2)}) copy-start(bf16[1536,256]{1,0:T(8,128)(2,1)} %constant.4.clone.table_ref) | copy-start | bytes 2359300
  8.9 2.8 %copy-start.2 = (bf16[1,32,4096]{2,1,0:T(8,128)(2,1)S(1)}, bf16[1,32,4096]{2,1,0:T(8,128)(2,1)}, u32[]{:S(2)}) copy-start(bf16[1,32,4096]{2,1,0:T(8,128)(2,1)} %param.4) | copy-start | bytes 786436
  9.0 6.6 %collective-permute-start.1 = (f32[64,128]{1,0:T(8,128)S(1)}, f32[64,128]{1,0:T(8,128)S(1)}, u32[]{:S(2)}, u32[]{:S(2)}) collective-permute-start(f32[64,128]{1,0:T(8,128)S(1)} %first_part.1), channel_id=1, source_target_pairs={{33,0},{34,1},{35,2},{36,3},{37,4},{38,5},{39,6},{40,7},{41,8},{42... | collective-permute-start | bytes 98312 | tf_op jit(solution)/shard_map/ppermute | solution.py:421
  10.4 5.1 %collective-permute-start = (f32[64,128]{1,0:T(8,128)S(1)}, f32[64,128]{1,0:T(8,128)S(1)}, u32[]{:S(2)}, u32[]{:S(2)}) collective-permute-start(f32[64,128]{1,0:T(8,128)S(1)} %first_part.1), channel_id=1, source_target_pairs={{1,0},{2,1},{3,2},{4,3},{5,4},{6,5},{7,6},{8,7},{9,8},{10,9},{11,1... | collective-permute-start | bytes 98312 | tf_op jit(solution)/shard_map/ppermute | solution.py:421
  16.9 18.3 %collective-permute-start.3 = (f32[2,64,1152]{2,1,0:T(8,128)S(1)}, f32[2,64,1152]{2,1,0:T(8,128)S(1)}, u32[]{:S(2)}, u32[]{:S(2)}) collective-permute-start(f32[2,64,1152]{2,1,0:T(8,128)S(1)} %get-tuple-element.26), channel_id=1, source_target_pairs={{0,32},{1,33},{2,34},{3,35},{4,36},{5,37},{6,38},{7,39},{8,40},{9,... | collective-permute-start | bytes 1769480 | tf_op jit(solution)/shard_map/ppermute | solution.py:421
  22.5 16.7 %all-to-all-start = ((f32[32,1,128]{2,1,0:T(1,128)}), f32[32,1,128]{2,1,0:T(1,128)S(1)}, u32[]{:S(2)}, u32[]{:S(2)}) async-start(f32[32,1,128]{2,1,0:T(1,128)} %get-tuple-element.27), calls=%async_computation | async-start | bytes 32768 | tf_op jit(solution)/shard_map/all_to_all | solution.py:434
  35.2 13.9 %collective-permute-start.4 = (f32[2,64,128]{2,1,0:T(8,128)S(1)}, f32[2,64,128]{2,1,0:T(8,128)S(1)}, u32[]{:S(2)}, u32[]{:S(2)}) collective-permute-start(f32[2,64,128]{2,1,0:T(8,128)S(1)} %slice_add_fusion), channel_id=1, source_target_pairs={{0,1},{1,2},{2,3},{3,4},{4,5},{5,6},{6,7},{7,8},{8,9},{9,10},{10,1... | collective-permute-start | bytes 196616 | tf_op jit(solution)/shard_map/ppermute | solution.py:421

commit v5 on v4

--- a/solution.py
+++ b/solution.py
@@ -253,6 +253,11 @@
             seam_ref[v, c * WIN:(c + 1) * WIN] = odd[7] + cols[7 * WIN:8 * WIN, lanes]
 
 
+def folded(product):
+    half = product.shape[0] // 2
+    return product[:half, :256] + product[half:, :256] + product[:half, 256:]
+
+
 def edge_kernel(
     right_ref, corner_ref, table_ref, levels_ref, grid_ref, last_ref, seam_ref, inner_sums_ref,
     own_ref, rows_ref, tail_ref, sums_hbm,
@@ -265,7 +270,12 @@
     def _():
         edge = by_rows(table_ref[BOTH, :], jnp.concatenate([right_ref[...], corner_ref[...]], axis=0))
         spread(back_by_stride([last_ref[...], edge]), high_ref, low_ref, 0)
-        real, imag, power, sums = spectra(high_ref, low_ref, levels, table_ref)
+        fields = jnp.concatenate([high_ref[...], low_ref[...]], axis=0)
+        table = jnp.concatenate([table_ref[COL_HIGH, :], table_ref[COL_LOW, :]], axis=1)
+        spectrum = folded(mul(fields, table))
+        real, imag = spectrum[:, :LANES], spectrum[:, LANES:]
+        power = real * real + imag * imag
+        sums = packed(power * power, levels * power)
         fields_ref[0], fields_ref[1], fields_ref[2] = real, imag, power
         row = inner_sums_ref[...] + sums
         copies_ref[...] = jnp.broadcast_to(row[None], copies_ref.shape)
@@ -274,8 +284,12 @@
     @pl.when(pl.program_id(0) == 1)
     def _():
         real, imag, power = fields_ref[0], fields_ref[1], fields_ref[2]
-        for v, factor in enumerate((power, levels)):
-            cols = adjoint_cols(real, imag, factor, table_ref)
+        weighted = [jnp.concatenate([real * factor, imag * factor], axis=1) for factor in (power, levels)]
+        fields = jnp.concatenate(split(jnp.concatenate(weighted, axis=0)), axis=0)
+        table = jnp.concatenate([table_ref[COL_HIGH, :], table_ref[COL_LOW, :]], axis=0)
+        both = folded(lax.dot_general(fields, table, (((1,), (1,)), ((), ())), preferred_element_type=F32))
+        for v in range(2):
+            cols = both[v * WIN:(v + 1) * WIN]
             for c in range(2):
                 seam, tail = turned([cols[:, c * LANES:(c + 1) * LANES]])
                 place(edge_ref, c, seam + seam_ref[v, c * WIN:(c + 1) * WIN], v * 2 * LANES)

time: 50.6 us -> 50.4 us (level)
  no operation moved by 1% of the time
where the time goes in v5:
time: 50.4 us; the launch traced here: 49.8 us
  starting transfers between devices  32.4 us (64%)
  blocking collectives  9.84 us (20%)
  Pallas kernels  4.31 us (9%)
  waiting for transfers between devices  3.04 us (6%)
    ppermute x5, starting transfers between devices, moved(): return lax.ppermute(block, AXES, route)  19.7 us
    all_to_all x1, starting transfers between devices, shared(): lax.all_to_all(copies, AXES, 0, 0, axis_index_groups=groups, tiled=True)  12.7 us
    all_to_all x1, blocking collectives, shared(): lax.all_to_all(copies, AXES, 0, 0, axis_index_groups=groups, tiled=True)  9.84 us
    pallas_call x1, Pallas kernels, inner_part(): pl.pallas_call(inner_kernel, out_shape=(pltpu.VMEM((256, 14 * LANES), BF1...  1.76 us
    ppermute x5, waiting for transfers between devices, moved(): return lax.ppermute(block, AXES, route)  1.61 us
    all_to_all x1, waiting for transfers between devices, shared(): lax.all_to_all(copies, AXES, 0, 0, axis_index_groups=groups, tiled=True)  1.43 us
    pallas_call x1, Pallas kernels, edge_part(): pl.pallas_call(edge_kernel, out_shape=(pltpu.VMEM((2, WIN, 1024), F32), p...  1.19 us
  transfers between devices with their start and end apart: 6, of which 2 were waited for; matrix products, arithmetic and copies ran while one was open for 0% of the time, Pallas kernels for 5%

profile of v5, /device:TPU:1, one launch (start us, length us, event | category | flops | bytes accessed | tf_op | source)
XLA Modules:
  0.0 49.8 jit_solution(1453344194925426073)
XLA Ops:
  0.0 0.0 copy-start.1
  0.0 8.9 %collective-permute-start.2 = (f32[64,1024]{1,0:T(8,128)}, f32[64,1024]{1,0:T(8,128)S(1)}, u32[]{:S(2)}, u32[]{:S(2)}) collective-permute-start(f32[64,1024]{1,0:T(8,128)} %bitcast.6), channel_id=1, source_target_pairs={{32,0},{33,1},{34,2},{35,3},{36,4},{37,5},{38,6},{39,7},{40,8},{41... | collective-permute-start | bytes 786440 | tf_op jit(solution)/shard_map/ppermute | solution.py:435
  8.9 0.0 copy-start
  8.9 0.0 copy-done.1
  8.9 0.0 copy-start.2
  9.0 1.4 %collective-permute-start.1 = (f32[64,128]{1,0:T(8,128)S(1)}, f32[64,128]{1,0:T(8,128)S(1)}, u32[]{:S(2)}, u32[]{:S(2)}) collective-permute-start(f32[64,128]{1,0:T(8,128)S(1)} %first_part.1), channel_id=1, source_target_pairs={{33,0},{34,1},{35,2},{36,3},{37,4},{38,5},{39,6},{40,7},{41,8},{42... | collective-permute-start | bytes 98312 | tf_op jit(solution)/shard_map/ppermute | solution.py:435
  10.4 1.3 %collective-permute-start = (f32[64,128]{1,0:T(8,128)S(1)}, f32[64,128]{1,0:T(8,128)S(1)}, u32[]{:S(2)}, u32[]{:S(2)}) collective-permute-start(f32[64,128]{1,0:T(8,128)S(1)} %first_part.1), channel_id=1, source_target_pairs={{1,0},{2,1},{3,2},{4,3},{5,4},{6,5},{7,6},{8,7},{9,8},{10,9},{11,1... | collective-permute-start | bytes 98312 | tf_op jit(solution)/shard_map/ppermute | solution.py:435
  11.7 0.0 copy-done
  11.7 0.0 copy-done.2
  11.7 0.4 local_part.1
  12.2 0.0 collective-permute-done.2.below_ref
  12.2 1.8 %inner_part.1 = (bf16[256,1792]{1,0:T(8,128)(2,1)S(1)}, f32[128,128]{1,0:T(8,128)S(1)}, f32[2,128,128]{2,1,0:T(8,128)S(1)}, f32[1,128]{1,0:T(1,128)S(1)}) custom-call(f32[64,1024]{1,0:T(8,128)S(1)} %collective-permute-done.2.below_ref, bf16[1536,256]{1,0:T(8,128)(2,1)S(1)} %copy-done, f32[1024,128]{1,0:T(8,128)S(1)} %get-tuple-element.18.levels_ref, ...), custom_call_target="tpu_custom_call" | custom-call | flops 1000000000 | bytes 5000000 | tf_op jit(solution)/shard_map/inner_part/pallas_call | solution.py:334
  14.0 1.6 %collective-permute-done.1.corner_ref = f32[64,128]{1,0:T(8,128)S(1)} collective-permute-done((f32[64,128]{1,0:T(8,128)S(1)}, f32[64,128]{1,0:T(8,128)S(1)}, u32[]{:S(2)}, u32[]{:S(2)}) %collective-permute-start.1) | collective-permute-done | bytes 32800 | tf_op jit(solution)/shard_map/ppermute | solution.py:435
  15.6 0.0 collective-permute-done.right_ref
  15.6 1.2 %edge_part.1 = (f32[2,64,1024]{2,1,0:T(8,128)S(1)}, f32[2,64,1152]{2,1,0:T(8,128)S(1)}, f32[2,64,128]{2,1,0:T(8,128)S(1)}, f32[32,1,128]{2,1,0:T(1,128)}) custom-call(f32[64,128]{1,0:T(8,128)S(1)} %collective-permute-done.right_ref, f32[64,128]{1,0:T(8,128)S(1)} %collective-permute-done.1.corner_ref, bf16[1536,256]{1,0:T(8,128)(2,1)S(1)} %copy-done, ...), custom_call_target="tpu_custom_call" | custom-call | flops 100000000 | bytes 2000000 | tf_op jit(solution)/shard_map/edge_part/pallas_call | solution.py:355
  16.8 5.6 %collective-permute-start.3 = (f32[2,64,1152]{2,1,0:T(8,128)S(1)}, f32[2,64,1152]{2,1,0:T(8,128)S(1)}, u32[]{:S(2)}, u32[]{:S(2)}) collective-permute-start(f32[2,64,1152]{2,1,0:T(8,128)S(1)} %get-tuple-element.26), channel_id=1, source_target_pairs={{0,32},{1,33},{2,34},{3,35},{4,36},{5,37},{6,38},{7,39},{8,40},{9,... | collective-permute-start | bytes 1769480 | tf_op jit(solution)/shard_map/ppermute | solution.py:435
  22.4 12.7 %all-to-all-start = ((f32[32,1,128]{2,1,0:T(1,128)}), f32[32,1,128]{2,1,0:T(1,128)S(1)}, u32[]{:S(2)}, u32[]{:S(2)}) async-start(f32[32,1,128]{2,1,0:T(1,128)} %get-tuple-element.27), calls=%async_computation | async-start | bytes 32768 | tf_op jit(solution)/shard_map/all_to_all | solution.py:448
  35.0 0.0 collective-permute-done.3.rows_ref
  35.1 2.5 %collective-permute-start.4 = (f32[2,64,128]{2,1,0:T(8,128)S(1)}, f32[2,64,128]{2,1,0:T(8,128)S(1)}, u32[]{:S(2)}, u32[]{:S(2)}) collective-permute-start(f32[2,64,128]{2,1,0:T(8,128)S(1)} %slice_add_fusion), channel_id=1, source_target_pairs={{0,1},{1,2},{2,3},{3,4},{4,5},{5,6},{6,7},{7,8},{8,9},{9,10},{10,1... | collective-permute-start | bytes 196616 | tf_op jit(solution)/shard_map/ppermute | solution.py:435
  37.6 1.4 %all-to-all-done = f32[32,1,128]{2,1,0:T(1,128)S(1)} async-done(((f32[32,1,128]{2,1,0:T(1,128)}), f32[32,1,128]{2,1,0:T(1,128)S(1)}, u32[]{:S(2)}, u32[]{:S(2)}) %all-to-all-start) | async-done | bytes 16416 | tf_op jit(solution)/shard_map/all_to_all | solution.py:448
  39.0 0.1 reduce_sum.11
  39.1 0.1 merge_part.1.both_ref
  39.1 9.8 %all_to_all.10 = f32[16,1,128]{2,1,0:T(1,128)S(1)} all-to-all(f32[16,1,128]{2,1,0:T(1,128)S(1)} %broadcast_in_dim.9), channel_id=1, replica_groups={{320,321,256,257,448,449,384,385,64,65,0,1,192,193,128,129},{322,323,25..., dimensions={0} | all-to-all | bytes 16384 | tf_op jit(solution)/shard_map/all_to_all | solution.py:448
  49.0 0.0 collective-permute-done.4.cols_ref
  49.0 0.9 %combine.1 = f32[64,1024]{1,0:T(8,128)} custom-call(f32[2,64,1024]{2,1,0:T(8,128)S(1)} %merge_part.1.both_ref, f32[2,64,128]{2,1,0:T(8,128)S(1)} %collective-permute-done.4.cols_ref, f32[64,1024]{1,0:T(8,128)S(1)} %bitcast.9, f32[16,128]{1,0:T(8,128)S(1)} %bitcast.11), custom_call_target="tpu_custom_call" | custom-call | flops 1000000 | bytes 2000000 | tf_op jit(solution)/shard_map/combine/pallas_call | solution.py:415
  (4 shorter events, 0.0 us)
Async XLA Ops:
  0.0 8.9 %copy-start.1 = (f32[2,32,1024]{2,1,0:T(8,128)S(1)}, f32[2,32,1024]{2,1,0:T(8,128)}, u32[]{:S(2)}) copy-start(f32[2,32,1024]{2,1,0:T(8,128)} %param.3) | copy-start | bytes 786436
  0.0 12.2 %collective-permute-start.2 = (f32[64,1024]{1,0:T(8,128)}, f32[64,1024]{1,0:T(8,128)S(1)}, u32[]{:S(2)}, u32[]{:S(2)}) collective-permute-start(f32[64,1024]{1,0:T(8,128)} %bitcast.6), channel_id=1, source_target_pairs={{32,0},{33,1},{34,2},{35,3},{36,4},{37,5},{38,6},{39,7},{40,8},{41... | collective-permute-start | bytes 786440 | tf_op jit(solution)/shard_map/ppermute | solution.py:435
  8.9 2.8 %copy-start = (bf16[1536,256]{1,0:T(8,128)(2,1)S(1)}, bf16[1536,256]{1,0:T(8,128)(2,1)}, u32[]{:S(2)}) copy-start(bf16[1536,256]{1,0:T(8,128)(2,1)} %constant.4.clone.table_ref) | copy-start | bytes 2359300
  8.9 2.8 %copy-start.2 = (bf16[1,32,4096]{2,1,0:T(8,128)(2,1)S(1)}, bf16[1,32,4096]{2,1,0:T(8,128)(2,1)}, u32[]{:S(2)}) copy-start(bf16[1,32,4096]{2,1,0:T(8,128)(2,1)} %param.4) | copy-start | bytes 786436
  9.0 6.6 %collective-permute-start.1 = (f32[64,128]{1,0:T(8,128)S(1)}, f32[64,128]{1,0:T(8,128)S(1)}, u32[]{:S(2)}, u32[]{:S(2)}) collective-permute-start(f32[64,128]{1,0:T(8,128)S(1)} %first_part.1), channel_id=1, source_target_pairs={{33,0},{34,1},{35,2},{36,3},{37,4},{38,5},{39,6},{40,7},{41,8},{42... | collective-permute-start | bytes 98312 | tf_op jit(solution)/shard_map/ppermute | solution.py:435
  10.4 5.1 %collective-permute-start = (f32[64,128]{1,0:T(8,128)S(1)}, f32[64,128]{1,0:T(8,128)S(1)}, u32[]{:S(2)}, u32[]{:S(2)}) collective-permute-start(f32[64,128]{1,0:T(8,128)S(1)} %first_part.1), channel_id=1, source_target_pairs={{1,0},{2,1},{3,2},{4,3},{5,4},{6,5},{7,6},{8,7},{9,8},{10,9},{11,1... | collective-permute-start | bytes 98312 | tf_op jit(solution)/shard_map/ppermute | solution.py:435
  16.8 18.3 %collective-permute-start.3 = (f32[2,64,1152]{2,1,0:T(8,128)S(1)}, f32[2,64,1152]{2,1,0:T(8,128)S(1)}, u32[]{:S(2)}, u32[]{:S(2)}) collective-permute-start(f32[2,64,1152]{2,1,0:T(8,128)S(1)} %get-tuple-element.26), channel_id=1, source_target_pairs={{0,32},{1,33},{2,34},{3,35},{4,36},{5,37},{6,38},{7,39},{8,40},{9,... | collective-permute-start | bytes 1769480 | tf_op jit(solution)/shard_map/ppermute | solution.py:435
  22.4 16.6 %all-to-all-start = ((f32[32,1,128]{2,1,0:T(1,128)}), f32[32,1,128]{2,1,0:T(1,128)S(1)}, u32[]{:S(2)}, u32[]{:S(2)}) async-start(f32[32,1,128]{2,1,0:T(1,128)} %get-tuple-element.27), calls=%async_computation | async-start | bytes 32768 | tf_op jit(solution)/shard_map/all_to_all | solution.py:448
  35.1 13.9 %collective-permute-start.4 = (f32[2,64,128]{2,1,0:T(8,128)S(1)}, f32[2,64,128]{2,1,0:T(8,128)S(1)}, u32[]{:S(2)}, u32[]{:S(2)}) collective-permute-start(f32[2,64,128]{2,1,0:T(8,128)S(1)} %slice_add_fusion), channel_id=1, source_target_pairs={{0,1},{1,2},{2,3},{3,4},{4,5},{5,6},{6,7},{7,8},{8,9},{9,10},{10,1... | collective-permute-start | bytes 196616 | tf_op jit(solution)/shard_map/ppermute | solution.py:435

commit v6 on v5

--- a/solution.py
+++ b/solution.py
@@ -269,8 +269,8 @@
     @pl.when(pl.program_id(0) == 0)
     def _():
         edge = by_rows(table_ref[BOTH, :], jnp.concatenate([right_ref[...], corner_ref[...]], axis=0))
-        spread(back_by_stride([last_ref[...], edge]), high_ref, low_ref, 0)
-        fields = jnp.concatenate([high_ref[...], low_ref[...]], axis=0)
+        pair = [jnp.concatenate([part[:WIN], part[WIN:]], axis=1) for part in split(back_by_stride([last_ref[...], edge])[0])]
+        fields = jnp.concatenate(pair, axis=0)
         table = jnp.concatenate([table_ref[COL_HIGH, :], table_ref[COL_LOW, :]], axis=1)
         spectrum = folded(mul(fields, table))
         real, imag = spectrum[:, :LANES], spectrum[:, LANES:]

time: 50.4 us -> 50.4 us (level)
  no operation moved by 1% of the time
where the time goes in v6:
time: 50.4 us; the launch traced here: 49.8 us
  starting transfers between devices  32.4 us (64%)
  blocking collectives  9.84 us (20%)
  Pallas kernels  4.31 us (9%)
  waiting for transfers between devices  3.04 us (6%)
    ppermute x5, starting transfers between devices, moved(): return lax.ppermute(block, AXES, route)  19.7 us
    all_to_all x1, starting transfers between devices, shared(): lax.all_to_all(copies, AXES, 0, 0, axis_index_groups=groups, tiled=True)  12.7 us
    all_to_all x1, blocking collectives, shared(): lax.all_to_all(copies, AXES, 0, 0, axis_index_groups=groups, tiled=True)  9.84 us
    pallas_call x1, Pallas kernels, inner_part(): pl.pallas_call(inner_kernel, out_shape=(pltpu.VMEM((256, 14 * LANES), BF1...  1.76 us
    ppermute x5, waiting for transfers between devices, moved(): return lax.ppermute(block, AXES, route)  1.61 us
    all_to_all x1, waiting for transfers between devices, shared(): lax.all_to_all(copies, AXES, 0, 0, axis_index_groups=groups, tiled=True)  1.43 us
    pallas_call x1, Pallas kernels, edge_part(): pl.pallas_call(edge_kernel, out_shape=(pltpu.VMEM((2, WIN, 1024), F32), p...  1.19 us
  transfers between devices with their start and end apart: 6, of which 2 were waited for; matrix products, arithmetic and copies ran while one was open for 0% of the time, Pallas kernels for 5%

profile of v6, /device:TPU:1, one launch (start us, length us, event | category | flops | bytes accessed | tf_op | source)
XLA Modules:
  0.0 49.8 jit_solution(18292623078403932858)
XLA Ops:
  0.0 0.0 copy-start.1
  0.0 8.9 %collective-permute-start.2 = (f32[64,1024]{1,0:T(8,128)}, f32[64,1024]{1,0:T(8,128)S(1)}, u32[]{:S(2)}, u32[]{:S(2)}) collective-permute-start(f32[64,1024]{1,0:T(8,128)} %bitcast.6), channel_id=1, source_target_pairs={{32,0},{33,1},{34,2},{35,3},{36,4},{37,5},{38,6},{39,7},{40,8},{41... | collective-permute-start | bytes 786440 | tf_op jit(solution)/shard_map/ppermute | solution.py:435
  8.9 0.0 copy-start
  8.9 0.0 copy-done.1
  8.9 0.0 copy-start.2
  9.0 1.4 %collective-permute-start.1 = (f32[64,128]{1,0:T(8,128)S(1)}, f32[64,128]{1,0:T(8,128)S(1)}, u32[]{:S(2)}, u32[]{:S(2)}) collective-permute-start(f32[64,128]{1,0:T(8,128)S(1)} %first_part.1), channel_id=1, source_target_pairs={{33,0},{34,1},{35,2},{36,3},{37,4},{38,5},{39,6},{40,7},{41,8},{42... | collective-permute-start | bytes 98312 | tf_op jit(solution)/shard_map/ppermute | solution.py:435
  10.4 1.3 %collective-permute-start = (f32[64,128]{1,0:T(8,128)S(1)}, f32[64,128]{1,0:T(8,128)S(1)}, u32[]{:S(2)}, u32[]{:S(2)}) collective-permute-start(f32[64,128]{1,0:T(8,128)S(1)} %first_part.1), channel_id=1, source_target_pairs={{1,0},{2,1},{3,2},{4,3},{5,4},{6,5},{7,6},{8,7},{9,8},{10,9},{11,1... | collective-permute-start | bytes 98312 | tf_op jit(solution)/shard_map/ppermute | solution.py:435
  11.7 0.0 copy-done
  11.7 0.0 copy-done.2
  11.7 0.4 local_part.1
  12.2 0.0 collective-permute-done.2.below_ref
  12.2 1.8 %inner_part.1 = (bf16[256,1792]{1,0:T(8,128)(2,1)S(1)}, f32[128,128]{1,0:T(8,128)S(1)}, f32[2,128,128]{2,1,0:T(8,128)S(1)}, f32[1,128]{1,0:T(1,128)S(1)}) custom-call(f32[64,1024]{1,0:T(8,128)S(1)} %collective-permute-done.2.below_ref, bf16[1536,256]{1,0:T(8,128)(2,1)S(1)} %copy-done, f32[1024,128]{1,0:T(8,128)S(1)} %get-tuple-element.18.levels_ref, ...), custom_call_target="tpu_custom_call" | custom-call | flops 1000000000 | bytes 5000000 | tf_op jit(solution)/shard_map/inner_part/pallas_call | solution.py:334
  14.0 1.6 %collective-permute-done.1.corner_ref = f32[64,128]{1,0:T(8,128)S(1)} collective-permute-done((f32[64,128]{1,0:T(8,128)S(1)}, f32[64,128]{1,0:T(8,128)S(1)}, u32[]{:S(2)}, u32[]{:S(2)}) %collective-permute-start.1) | collective-permute-done | bytes 32800 | tf_op jit(solution)/shard_map/ppermute | solution.py:435
  15.6 0.0 collective-permute-done.right_ref
  15.6 1.2 %edge_part.1 = (f32[2,64,1024]{2,1,0:T(8,128)S(1)}, f32[2,64,1152]{2,1,0:T(8,128)S(1)}, f32[2,64,128]{2,1,0:T(8,128)S(1)}, f32[32,1,128]{2,1,0:T(1,128)}) custom-call(f32[64,128]{1,0:T(8,128)S(1)} %collective-permute-done.right_ref, f32[64,128]{1,0:T(8,128)S(1)} %collective-permute-done.1.corner_ref, bf16[1536,256]{1,0:T(8,128)(2,1)S(1)} %copy-done, ...), custom_call_target="tpu_custom_call" | custom-call | flops 100000000 | bytes 2000000 | tf_op jit(solution)/shard_map/edge_part/pallas_call | solution.py:355
  16.8 5.6 %collective-permute-start.3 = (f32[2,64,1152]{2,1,0:T(8,128)S(1)}, f32[2,64,1152]{2,1,0:T(8,128)S(1)}, u32[]{:S(2)}, u32[]{:S(2)}) collective-permute-start(f32[2,64,1152]{2,1,0:T(8,128)S(1)} %get-tuple-element.26), channel_id=1, source_target_pairs={{0,32},{1,33},{2,34},{3,35},{4,36},{5,37},{6,38},{7,39},{8,40},{9,... | collective-permute-start | bytes 1769480 | tf_op jit(solution)/shard_map/ppermute | solution.py:435
  22.3 12.7 %all-to-all-start = ((f32[32,1,128]{2,1,0:T(1,128)}), f32[32,1,128]{2,1,0:T(1,128)S(1)}, u32[]{:S(2)}, u32[]{:S(2)}) async-start(f32[32,1,128]{2,1,0:T(1,128)} %get-tuple-element.27), calls=%async_computation | async-start | bytes 32768 | tf_op jit(solution)/shard_map/all_to_all | solution.py:448
  35.0 0.0 collective-permute-done.3.rows_ref
  35.1 2.5 %collective-permute-start.4 = (f32[2,64,128]{2,1,0:T(8,128)S(1)}, f32[2,64,128]{2,1,0:T(8,128)S(1)}, u32[]{:S(2)}, u32[]{:S(2)}) collective-permute-start(f32[2,64,128]{2,1,0:T(8,128)S(1)} %slice_add_fusion), channel_id=1, source_target_pairs={{0,1},{1,2},{2,3},{3,4},{4,5},{5,6},{6,7},{7,8},{8,9},{9,10},{10,1... | collective-permute-start | bytes 196616 | tf_op jit(solution)/shard_map/ppermute | solution.py:435
  37.6 1.4 %all-to-all-done = f32[32,1,128]{2,1,0:T(1,128)S(1)} async-done(((f32[32,1,128]{2,1,0:T(1,128)}), f32[32,1,128]{2,1,0:T(1,128)S(1)}, u32[]{:S(2)}, u32[]{:S(2)}) %all-to-all-start) | async-done | bytes 16416 | tf_op jit(solution)/shard_map/all_to_all | solution.py:448
  39.0 0.1 reduce_sum.11
  39.1 0.1 merge_part.1.both_ref
  39.1 9.8 %all_to_all.10 = f32[16,1,128]{2,1,0:T(1,128)S(1)} all-to-all(f32[16,1,128]{2,1,0:T(1,128)S(1)} %broadcast_in_dim.9), channel_id=1, replica_groups={{320,321,256,257,448,449,384,385,64,65,0,1,192,193,128,129},{322,323,25..., dimensions={0} | all-to-all | bytes 16384 | tf_op jit(solution)/shard_map/all_to_all | solution.py:448
  49.0 0.0 collective-permute-done.4.cols_ref
  49.0 0.9 %combine.1 = f32[64,1024]{1,0:T(8,128)} custom-call(f32[2,64,1024]{2,1,0:T(8,128)S(1)} %merge_part.1.both_ref, f32[2,64,128]{2,1,0:T(8,128)S(1)} %collective-permute-done.4.cols_ref, f32[64,1024]{1,0:T(8,128)S(1)} %bitcast.9, f32[16,128]{1,0:T(8,128)S(1)} %bitcast.11), custom_call_target="tpu_custom_call" | custom-call | flops 1000000 | bytes 2000000 | tf_op jit(solution)/shard_map/combine/pallas_call | solution.py:415
  (4 shorter events, 0.0 us)
Async XLA Ops:
  0.0 8.9 %copy-start.1 = (f32[2,32,1024]{2,1,0:T(8,128)S(1)}, f32[2,32,1024]{2,1,0:T(8,128)}, u32[]{:S(2)}) copy-start(f32[2,32,1024]{2,1,0:T(8,128)} %param.3) | copy-start | bytes 786436
  0.0 12.2 %collective-permute-start.2 = (f32[64,1024]{1,0:T(8,128)}, f32[64,1024]{1,0:T(8,128)S(1)}, u32[]{:S(2)}, u32[]{:S(2)}) collective-permute-start(f32[64,1024]{1,0:T(8,128)} %bitcast.6), channel_id=1, source_target_pairs={{32,0},{33,1},{34,2},{35,3},{36,4},{37,5},{38,6},{39,7},{40,8},{41... | collective-permute-start | bytes 786440 | tf_op jit(solution)/shard_map/ppermute | solution.py:435
  8.9 2.8 %copy-start = (bf16[1536,256]{1,0:T(8,128)(2,1)S(1)}, bf16[1536,256]{1,0:T(8,128)(2,1)}, u32[]{:S(2)}) copy-start(bf16[1536,256]{1,0:T(8,128)(2,1)} %constant.4.clone.table_ref) | copy-start | bytes 2359300
  8.9 2.8 %copy-start.2 = (bf16[1,32,4096]{2,1,0:T(8,128)(2,1)S(1)}, bf16[1,32,4096]{2,1,0:T(8,128)(2,1)}, u32[]{:S(2)}) copy-start(bf16[1,32,4096]{2,1,0:T(8,128)(2,1)} %param.4) | copy-start | bytes 786436
  9.0 6.6 %collective-permute-start.1 = (f32[64,128]{1,0:T(8,128)S(1)}, f32[64,128]{1,0:T(8,128)S(1)}, u32[]{:S(2)}, u32[]{:S(2)}) collective-permute-start(f32[64,128]{1,0:T(8,128)S(1)} %first_part.1), channel_id=1, source_target_pairs={{33,0},{34,1},{35,2},{36,3},{37,4},{38,5},{39,6},{40,7},{41,8},{42... | collective-permute-start | bytes 98312 | tf_op jit(solution)/shard_map/ppermute | solution.py:435
  10.4 5.1 %collective-permute-start = (f32[64,128]{1,0:T(8,128)S(1)}, f32[64,128]{1,0:T(8,128)S(1)}, u32[]{:S(2)}, u32[]{:S(2)}) collective-permute-start(f32[64,128]{1,0:T(8,128)S(1)} %first_part.1), channel_id=1, source_target_pairs={{1,0},{2,1},{3,2},{4,3},{5,4},{6,5},{7,6},{8,7},{9,8},{10,9},{11,1... | collective-permute-start | bytes 98312 | tf_op jit(solution)/shard_map/ppermute | solution.py:435
  16.8 18.3 %collective-permute-start.3 = (f32[2,64,1152]{2,1,0:T(8,128)S(1)}, f32[2,64,1152]{2,1,0:T(8,128)S(1)}, u32[]{:S(2)}, u32[]{:S(2)}) collective-permute-start(f32[2,64,1152]{2,1,0:T(8,128)S(1)} %get-tuple-element.26), channel_id=1, source_target_pairs={{0,32},{1,33},{2,34},{3,35},{4,36},{5,37},{6,38},{7,39},{8,40},{9,... | collective-permute-start | bytes 1769480 | tf_op jit(solution)/shard_map/ppermute | solution.py:435
  22.3 16.7 %all-to-all-start = ((f32[32,1,128]{2,1,0:T(1,128)}), f32[32,1,128]{2,1,0:T(1,128)S(1)}, u32[]{:S(2)}, u32[]{:S(2)}) async-start(f32[32,1,128]{2,1,0:T(1,128)} %get-tuple-element.27), calls=%async_computation | async-start | bytes 32768 | tf_op jit(solution)/shard_map/all_to_all | solution.py:448
  35.1 13.9 %collective-permute-start.4 = (f32[2,64,128]{2,1,0:T(8,128)S(1)}, f32[2,64,128]{2,1,0:T(8,128)S(1)}, u32[]{:S(2)}, u32[]{:S(2)}) collective-permute-start(f32[2,64,128]{2,1,0:T(8,128)S(1)} %slice_add_fusion), channel_id=1, source_target_pairs={{0,1},{1,2},{2,3},{3,4},{4,5},{5,6},{6,7},{7,8},{8,9},{9,10},{10,1... | collective-permute-start | bytes 196616 | tf_op jit(solution)/shard_map/ppermute | solution.py:435
